TPU v7x, 128 devices: a whole 4x4x4 slice. The times are simulated.
128 devices in a mesh: grp: 8 (over y_lo, z), col: 16 (over y_hi, x, core).
Axes of the slice: x: 4, y: 4 (y_hi: 2, y_lo: 2; y = y_hi * 2 + y_lo), z: 4, core: 2. Of those that a mesh axis runs over, the one named last changes fastest.
Arguments:
- tokens: bfloat16 [1024, 6144], P('grp', 'col'), may hold values from -6 to 6
- grad_out: bfloat16 [1024, 6144], P('grp', 'col'), may hold values from -6 to 6
- expert_ids: int32 [1024, 2], P('grp'), may hold values from 0 to 3, all different within a row; in each aligned block of 128 rows (0 to 127, 128 to 255, ...) at most 80 rows name the same one
- gate_num: int32 [1024], P('grp'), may hold values from 1 to 63
- gate_weight: bfloat16 [6144, 32768], P(None, ('grp', 'col')), may hold values from -0.078125 to 0.078125
- up_weight: bfloat16 [6144, 32768], P(None, ('grp', 'col')), may hold values from -0.078125 to 0.078125
- down_weight: bfloat16 [32768, 6144], P(('grp', 'col')), may hold values from -0.0625 to 0.0625
Outputs:
- layer_out: bfloat16 [1024, 6144], P('grp', 'col')
- grad_tokens: bfloat16 [1024, 6144], P('grp', 'col')
- grad_gate: bfloat16 [6144, 32768], P(None, ('grp', 'col'))
- grad_up: bfloat16 [6144, 32768], P(None, ('grp', 'col'))
- grad_down: bfloat16 [32768, 6144], P(('grp', 'col'))
Inputs may be any that keep to these rules, and one draw needn't show every extreme that they name: `expert_ids`: the two ids of a token differ. In each aligned block of 128 tokens (those of one grp index) no expert is named by more than 80 tokens, a bound that some block reaches.
All inputs are finite; a program needn't handle non-finite values.
Results may differ from a plain program's by a relative error of at most 0.02.
Values may be sent and summed in bfloat16 or wider, within the bound.
A program may use at most 192 MiB of HBM per device.

v0:
```python
import jax
import jax.numpy as jnp
from jax import lax
from jax.sharding import PartitionSpec as P

SPAN = 2


def routing_tables(expert_ids, gate_num, experts, capacity):
    count = expert_ids.shape[0]
    flat_ids = expert_ids.reshape(-1)
    labels = jnp.arange(experts, dtype=jnp.int32)
    onehot = (flat_ids[:, None] == labels[None, :]).astype(jnp.int32)
    earlier = jnp.cumsum(onehot, axis=0) - onehot
    position = jnp.sum(earlier * onehot, axis=1)
    target = flat_ids * capacity + position
    share = gate_num.astype(jnp.float32) / 64.0
    pair_weight = jnp.stack([share, 1.0 - share], axis=1).reshape(-1)
    slots = jnp.arange(experts * capacity, dtype=jnp.int32)
    matches = slots[:, None] == target[None, :]
    chosen = jnp.any(matches.reshape(experts * capacity, count, 2), axis=2)
    weighted = jnp.where(matches, pair_weight[None, :], jnp.zeros_like(pair_weight)[None, :])
    slot_weight = jnp.sum(weighted, axis=1)
    return (target, pair_weight, chosen, slot_weight)


def dispatch(chosen, slot_weight, features, grads, experts, capacity):
    picker = chosen.astype(jnp.bfloat16)
    width = features.shape[1]
    moved = jnp.dot(picker, features, preferred_element_type=jnp.float32).astype(jnp.bfloat16)
    scaled = jnp.dot(picker, grads, preferred_element_type=jnp.float32) * slot_weight[:, None]
    scaled = scaled.astype(jnp.bfloat16)
    moved = jnp.repeat(moved.reshape(experts, capacity, width), SPAN, axis=0)
    scaled = jnp.repeat(scaled.reshape(experts, capacity, width), SPAN, axis=0)
    return (moved, scaled)


def combine(buffer, target, pair_weight, count):
    picked = jnp.take(buffer, target, axis=0)
    return jnp.sum(picked.reshape(count, 2, -1) * pair_weight.reshape(count, 2, 1), axis=1)


def body(tokens, grad_out, expert_ids, gate_num, gate_weight, up_weight, down_weight):
    groups = lax.axis_size("grp")
    experts = groups // SPAN
    count = tokens.shape[0]
    capacity = min(count, 5 * count // (2 * experts))
    target, pair_weight, chosen, slot_weight = routing_tables(
        expert_ids, gate_num, experts, capacity
    )
    whole_tokens, whole_grads = (
        lax.all_gather(tokens, "col", axis=1, tiled=True),
        lax.all_gather(grad_out, "col", axis=1, tiled=True),
    )
    sent_rows, sent_grads = dispatch(
        chosen, slot_weight, whole_tokens, whole_grads, experts, capacity
    )
    token_rows, grad_rows = (
        lax.all_to_all(sent_rows, "grp", split_axis=0, concat_axis=0, tiled=True),
        lax.all_to_all(sent_grads, "grp", split_axis=0, concat_axis=0, tiled=True),
    )
    width = token_rows.shape[2]
    token_rows = token_rows.reshape(groups * capacity, width)
    grad_rows = grad_rows.reshape(groups * capacity, width)
    gate_act = jnp.dot(token_rows, gate_weight, preferred_element_type=jnp.float32)
    up_act = jnp.dot(token_rows, up_weight, preferred_element_type=jnp.float32)
    sigmoid_gate = jax.nn.sigmoid(gate_act)
    hidden = (gate_act * sigmoid_gate * up_act).astype(jnp.bfloat16)
    out_part = jnp.dot(hidden, down_weight, preferred_element_type=jnp.float32)
    grad_hidden = lax.dot_general(
        grad_rows, down_weight, (((1,), (1,)), ((), ())), preferred_element_type=jnp.float32
    )
    grad_gate_act = (
        grad_hidden * up_act * sigmoid_gate * (1.0 + gate_act * (1.0 - sigmoid_gate))
    ).astype(jnp.bfloat16)
    grad_up_act = (grad_hidden * gate_act * sigmoid_gate).astype(jnp.bfloat16)
    contract_rows = (((0,), (0,)), ((), ()))
    grad_down = lax.dot_general(
        hidden, grad_rows, contract_rows, preferred_element_type=jnp.float32
    ).astype(jnp.bfloat16)
    grad_gate = lax.dot_general(
        token_rows, grad_gate_act, contract_rows, preferred_element_type=jnp.float32
    ).astype(jnp.bfloat16)
    grad_up = lax.dot_general(
        token_rows, grad_up_act, contract_rows, preferred_element_type=jnp.float32
    ).astype(jnp.bfloat16)
    contract_units = (((1,), (1,)), ((), ()))
    back_part = lax.dot_general(
        grad_gate_act, gate_weight, contract_units, preferred_element_type=jnp.float32
    )
    back_part = back_part + lax.dot_general(
        grad_up_act, up_weight, contract_units, preferred_element_type=jnp.float32
    )
    out_sums, back_sums = (
        lax.psum_scatter(
            out_part.reshape(groups, capacity, width).astype(jnp.bfloat16),
            "col",
            scatter_dimension=2,
            tiled=True,
        ).astype(jnp.float32),
        lax.psum_scatter(
            back_part.reshape(groups, capacity, width).astype(jnp.bfloat16),
            "col",
            scatter_dimension=2,
            tiled=True,
        ).astype(jnp.float32),
    )
    out_home, back_home = (
        lax.all_to_all(
            out_sums.astype(jnp.bfloat16), "grp", split_axis=0, concat_axis=0, tiled=True
        ).astype(out_sums.dtype),
        lax.all_to_all(
            back_sums.astype(jnp.bfloat16), "grp", split_axis=0, concat_axis=0, tiled=True
        ).astype(back_sums.dtype),
    )
    narrow = out_home.shape[2]
    out_buffer = jnp.sum(out_home.reshape(experts, SPAN, capacity, narrow), axis=1).reshape(
        experts * capacity, narrow
    )
    back_buffer = jnp.sum(back_home.reshape(experts, SPAN, capacity, narrow), axis=1).reshape(
        experts * capacity, narrow
    )
    layer_out = combine(out_buffer, target, pair_weight, count).astype(jnp.bfloat16)
    grad_tokens = combine(back_buffer, target, jnp.ones_like(pair_weight), count).astype(
        jnp.bfloat16
    )
    return (layer_out, grad_tokens, grad_gate, grad_up, grad_down)


def solution(mesh):
    placed = (
        P("grp", "col"),
        P("grp", "col"),
        P("grp", None),
        P("grp"),
        P(None, ("grp", "col")),
        P(None, ("grp", "col")),
        P(("grp", "col"), None),
    )
    return jax.shard_map(
        body,
        mesh=mesh,
        in_specs=placed,
        out_specs=(
            P("grp", "col"),
            P("grp", "col"),
            P(None, ("grp", "col")),
            P(None, ("grp", "col")),
            P(("grp", "col"), None),
        ),
        check_vma=False,
    )
```

profile of v0, /device:TPU:0, one launch (start us, length us, event | category | flops | bytes accessed | tf_op | source)
XLA Modules:
  0.0 543.2 jit_solution(11571511246859901053)
XLA Ops:
  11.8 48.4 %all-gather.3.cloned.1.call-done = bf16[128,6144]{1,0:T(8,128)(2,1)} async-done(((bf16[128,384]{1,0:T(8,128)(2,1)}), bf16[128,6144]{1,0:T(8,128)(2,1)}) %all-gather.3.cloned.1.call-update) | async-done | bytes 1572880 | tf_op jit(solution)/shard_map/all_gather | solution.py:52
  60.2 2.6 convolution_convert_fusion.1
  62.8 4.2 broadcast_in_dim.37
  67.0 5.1 all-to-all-start
  73.3 53.3 %all-gather.5.cloned.1.call-done = bf16[128,6144]{1,0:T(8,128)(2,1)} async-done(((bf16[128,384]{1,0:T(8,128)(2,1)}), bf16[128,6144]{1,0:T(8,128)(2,1)}) %all-gather.5.cloned.1.call-update) | async-done | bytes 1572880 | tf_op jit(solution)/shard_map/all_gather | solution.py:53
  126.6 4.6 fusion
  131.1 33.6 %all-to-all-done = bf16[8,80,6144]{2,1,0:T(8,128)(2,1)} async-done(((bf16[8,80,6144]{2,1,0:T(8,128)(2,1)}), bf16[8,80,6144]{2,1,0:T(8,128)(2,1)}, u32[]{:S(2)}, u32[]{:S(2)}) %all-to-all-start) | async-done | bytes 7864352 | tf_op jit(solution)/shard_map/all_to_all | solution.py:59
  164.7 6.2 %broadcast_in_dim.41 = bf16[4,2,80,6144]{3,2,1,0:T(8,128)(2,1)} broadcast(bf16[4,80,6144]{2,1,0:T(8,128)(2,1)} %bitcast.73), dimensions={0,2,3} | broadcast | bytes 11796480 | tf_op jit(solution)/shard_map/broadcast_in_dim | solution.py:34
  170.9 4.9 all-to-all-start.2
  176.1 7.3 %fusion.7 = f32[640,256]{1,0:T(8,128)} fusion(bf16[640,6144]{1,0:T(8,128)(2,1)} %bitcast.4, bf16[6144,256]{1,0:T(8,128)(2,1)} %param.14), kind=kOutput, calls=%fused_computation.40 | convolution fusion | flops 2013265920 | bytes 11665408 | tf_op jit(solution)/shard_map/dot_general | solution.py:66
  183.4 6.3 %fusion.6 = f32[640,256]{1,0:T(8,128)} fusion(bf16[640,6144]{1,0:T(8,128)(2,1)} %bitcast.4, bf16[6144,256]{1,0:T(8,128)(2,1)S(1)} %copy-done.3), kind=kOutput, calls=%fused_computation.39 | convolution fusion | flops 2013265920 | bytes 11665408 | tf_op jit(solution)/shard_map/dot_general | solution.py:65
  189.7 74.0 %all-to-all-done.2 = bf16[8,80,6144]{2,1,0:T(8,128)(2,1)} async-done(((bf16[8,80,6144]{2,1,0:T(8,128)(2,1)}), bf16[8,80,6144]{2,1,0:T(8,128)(2,1)}, u32[]{:S(2)}, u32[]{:S(2)}) %all-to-all-start.2) | async-done | bytes 7864352 | tf_op jit(solution)/shard_map/all_to_all | solution.py:60
  263.6 6.7 %multiply_convert_fusion = (bf16[640,256]{1,0:T(8,128)(2,1)}, bf16[640,256]{1,0:T(8,128)(2,1)}, bf16[640,256]{1,0:T(8,128)(2,1)S(1)}) fusion(f32[640,256]{1,0:T(8,128)} %fusion.6, f32[640,256]{1,0:T(8,128)} %fusion.7, bf16[640,6144]{1,0:T(8,128)(2,1)} %bitcast.12, bf16[256,6144]{1,0:T(8,128)(2,1)S(1)} %copy-done), kind=kOutput, calls=%fused_computation.12 | convolution fusion | flops 2015887360 | bytes 13303808 | tf_op jit(solution)/shard_map/dot_general | solution.py:70
  270.4 5.4 convolution_convert_fusion
  275.8 15.5 %copy.48 = bf16[8,80,6144]{1,0,2:T(8,128)(2,1)} copy(bf16[8,80,6144]{2,1,0:T(8,128)(2,1)} %bitcast.67) | data formatting | bytes 15728640
  291.3 18.8 %reshape.141 = bf16[6144,640]{1,0:T(8,128)(2,1)} reshape(bf16[6144,8,80]{2,1,0:T(8,128)(2,1)} %bitcast.65) | data formatting | bytes 15728640
  310.5 11.1 %fusion.8 = f32[640,6144]{1,0:T(8,128)} fusion(bf16[640,256]{1,0:T(8,128)(2,1)} %get-tuple-element.9, bf16[6144,256]{1,0:T(8,128)(2,1)} %param.13), kind=kOutput, calls=%fused_computation.41 | convolution fusion | flops 2013265920 | bytes 19202048 | tf_op jit(solution)/shard_map/dot_general | solution.py:88
  321.6 12.5 %add_convert_fusion = bf16[640,6144]{1,0:T(8,128)(2,1)} fusion(f32[640,6144]{1,0:T(8,128)} %fusion.8, bf16[640,256]{1,0:T(8,128)(2,1)S(1)} %copy-done.6, bf16[6144,256]{1,0:T(8,128)(2,1)S(1)} %copy-done.2), kind=kOutput, calls=%fused_computation.2 | convolution fusion | flops 2021130240 | bytes 27066368 | tf_op jit(solution)/shard_map/dot_general | solution.py:91
  334.0 15.8 %copy.50 = bf16[8,80,6144]{1,0,2:T(8,128)(2,1)} copy(bf16[8,80,6144]{2,1,0:T(8,128)(2,1)} %bitcast.70) | data formatting | bytes 15728640
  349.8 18.8 %reshape.143 = bf16[6144,640]{1,0:T(8,128)(2,1)} reshape(bf16[6144,8,80]{2,1,0:T(8,128)(2,1)} %bitcast.66) | data formatting | bytes 15728640
  369.6 8.0 %convolution_convert_fusion.3 = bf16[6144,256]{1,0:T(8,128)(2,1)} fusion(bf16[640,6144]{1,0:T(8,128)(2,1)} %bitcast.4, bf16[640,256]{1,0:T(8,128)(2,1)S(1)} %copy-done.7), kind=kOutput, calls=%fused_computation.8 | convolution fusion | flops 2014838784 | bytes 11337728 | tf_op jit(solution)/shard_map/dot_general | solution.py:84
  377.6 26.8 %reduce-scatter.7.cloned.1.call-done = bf16[384,640]{1,0:T(8,128)(2,1)} async-done(((bf16[6144,640]{1,0:T(8,128)(2,1)}), bf16[384,640]{1,0:T(8,128)(2,1)}) %reduce-scatter.7.cloned.1.call-update) | async-done | bytes 491536
  407.6 4.5 all-to-all-start.1
  412.1 7.6 %convolution_convert_fusion.4 = bf16[6144,256]{1,0:T(8,128)(2,1)} fusion(bf16[640,6144]{1,0:T(8,128)(2,1)} %bitcast.4, bf16[640,256]{1,0:T(8,128)(2,1)S(1)} %copy-done.5), kind=kOutput, calls=%fused_computation.9 | convolution fusion | flops 2014838784 | bytes 11337728 | tf_op jit(solution)/shard_map/dot_general | solution.py:81
  419.6 84.4 %reduce-scatter.9.cloned.1.call-done = bf16[384,640]{1,0:T(8,128)(2,1)} async-done(((bf16[6144,640]{1,0:T(8,128)(2,1)}), bf16[384,640]{1,0:T(8,128)(2,1)}) %reduce-scatter.9.cloned.1.call-update) | async-done | bytes 491536
  507.3 4.5 all-to-all-start.3
  511.8 7.3 %convolution_convert_fusion.2 = bf16[256,6144]{1,0:T(8,128)(2,1)} fusion(bf16[640,256]{1,0:T(8,128)(2,1)S(1)} %get-tuple-element.10, bf16[640,6144]{1,0:T(8,128)(2,1)} %bitcast.12), kind=kOutput, calls=%fused_computation.7 | convolution fusion | flops 2014838784 | bytes 11337728 | tf_op jit(solution)/shard_map/dot_general | solution.py:78
  519.1 2.1 convert_reduce_fusion.1
  521.1 2.2 gather_fusion
  525.3 2.9 gather_fusion.1
  528.2 2.0 broadcast_select_fusion
  533.4 2.2 multiply_reduce_fusion
  (60 shorter events, 19.9 us)
Async XLA Ops:
  7.2 256.5 %copy-start = (bf16[256,6144]{1,0:T(8,128)(2,1)S(1)}, bf16[256,6144]{1,0:T(8,128)(2,1)}, u32[]{:S(2)}) copy-start(bf16[256,6144]{1,0:T(8,128)(2,1)} %param.15) | copy-start | bytes 9437188
  7.2 53.0 %all-gather.3.cloned.1.call-start = ((), (), s32[]{:S(2)}) async-start(), calls=%async_computation.6 | async-start | bytes 1671168 | tf_op jit(solution)/shard_map/all_gather | solution.py:52
  67.0 5.8 %copy-start.8 = (s32[128]{0:T(128)S(1)}, s32[128]{0:T(128)}, u32[]{:S(2)}) copy-start(s32[128]{0:T(128)} %param.12) | copy-start | bytes 1540
  67.0 97.7 %all-to-all-start = ((bf16[8,80,6144]{2,1,0:T(8,128)(2,1)}), bf16[8,80,6144]{2,1,0:T(8,128)(2,1)}, u32[]{:S(2)}, u32[]{:S(2)}) async-start(bf16[8,80,6144]{2,1,0:T(8,128)(2,1)} %bitcast.68), calls=%async_computation | async-start | bytes 15728640 | tf_op jit(solution)/shard_map/all_to_all | solution.py:59
  72.1 54.5 %all-gather.5.cloned.1.call-start = ((), (), s32[]{:S(2)}) async-start(), calls=%async_computation.7 | async-start | bytes 1671168 | tf_op jit(solution)/shard_map/all_gather | solution.py:53
  73.0 97.9 %copy-start.4 = (f32[128,2]{1,0:T(8,128)}, f32[128,2]{1,0:T(8,128)S(1)}, u32[]{:S(2)}) copy-start(f32[128,2]{1,0:T(8,128)S(1)} %copy.46) | copy-start | bytes 3076
  170.9 92.7 %all-to-all-start.2 = ((bf16[8,80,6144]{2,1,0:T(8,128)(2,1)}), bf16[8,80,6144]{2,1,0:T(8,128)(2,1)}, u32[]{:S(2)}, u32[]{:S(2)}) async-start(bf16[8,80,6144]{2,1,0:T(8,128)(2,1)} %bitcast.69), calls=%async_computation.2 | async-start | bytes 15728640 | tf_op jit(solution)/shard_map/all_to_all | solution.py:60
  175.8 228.6 %reduce-scatter.7.cloned.1.call-start = ((), (), s32[]{:S(2)}) async-start(), calls=%async_computation.8 | async-start | bytes 8355840
  176.0 7.3 %copy-start.3 = (bf16[6144,256]{1,0:T(8,128)(2,1)S(1)}, bf16[6144,256]{1,0:T(8,128)(2,1)}, u32[]{:S(2)}) copy-start(bf16[6144,256]{1,0:T(8,128)(2,1)} %param.13) | copy-start | bytes 9437188
  310.2 193.9 %reduce-scatter.9.cloned.1.call-start = ((), (), s32[]{:S(2)}) async-start(), calls=%async_computation.9 | async-start | bytes 8355840
  310.4 11.1 %copy-start.2 = (bf16[6144,256]{1,0:T(8,128)(2,1)S(1)}, bf16[6144,256]{1,0:T(8,128)(2,1)}, u32[]{:S(2)}) copy-start(bf16[6144,256]{1,0:T(8,128)(2,1)} %param.14) | copy-start | bytes 9437188
  310.4 11.1 %copy-start.6 = (bf16[640,256]{1,0:T(8,128)(2,1)S(1)}, bf16[640,256]{1,0:T(8,128)(2,1)}, u32[]{:S(2)}) copy-start(bf16[640,256]{1,0:T(8,128)(2,1)} %get-tuple-element.8) | copy-start | bytes 983044
  368.6 1.0 copy-start.7
  369.6 42.5 %copy-start.5 = (bf16[640,256]{1,0:T(8,128)(2,1)S(1)}, bf16[640,256]{1,0:T(8,128)(2,1)}, u32[]{:S(2)}) copy-start(bf16[640,256]{1,0:T(8,128)(2,1)} %get-tuple-element.9) | copy-start | bytes 983044
  407.6 99.7 %all-to-all-start.1 = ((bf16[8,80,384]{2,1,0:T(8,128)(2,1)}), bf16[8,80,384]{2,1,0:T(8,128)(2,1)}, u32[]{:S(2)}, u32[]{:S(2)}) async-start(bf16[8,80,384]{2,1,0:T(8,128)(2,1)} %copy.49), calls=%async_computation.1 | async-start | bytes 983040 | tf_op jit(solution)/shard_map/all_to_all | solution.py:109
  507.3 16.0 %all-to-all-start.3 = ((bf16[8,80,384]{2,1,0:T(8,128)(2,1)}), bf16[8,80,384]{2,1,0:T(8,128)(2,1)}, u32[]{:S(2)}, u32[]{:S(2)}) async-start(bf16[8,80,384]{2,1,0:T(8,128)(2,1)} %copy.51), calls=%async_computation.3 | async-start | bytes 983040 | tf_op jit(solution)/shard_map/all_to_all | solution.py:112
  519.1 17.6 %copy-start.1 = (bf16[256,6144]{1,0:T(8,128)(2,1)S(1)}, bf16[256,6144]{1,0:T(8,128)(2,1)}, u32[]{:S(2)}) copy-start(bf16[256,6144]{1,0:T(8,128)(2,1)} %param.15) | copy-start | bytes 9437188
Sparse Core Ops, SparseCore 0:
  10.3 49.8 all-gather.2
  75.2 51.3 all-gather.4
  310.3 94.0 reduce-scatter.6
  408.5 95.5 reduce-scatter.8
where the time goes:
time: 546 us; the launch traced here: 543 us
  waiting for transfers between devices  322 us (59%)
  local copies, waits for them, and re-layouts  97 us (18%)
  matrix products  79.3 us (15%)
  starting transfers between devices  19.4 us (4%)
  between operations  14 us (3%)
  other arithmetic  11.6 us (2%)
    unnamed x6, waiting for transfers between devices  113 us
    unnamed x27, local copies, waits for them, and re-layouts  77.3 us
    all_to_all x1, waiting for transfers between devices, body(): lax.all_to_all(sent_grads, 'grp', split_axis=0, concat_axis=0, tiled=True)  74 us
    all_gather x1, waiting for transfers between devices, body(): lax.all_gather(grad_out, 'col', axis=1, tiled=True)  53.3 us
    all_gather x1, waiting for transfers between devices, body(): lax.all_gather(tokens, 'col', axis=1, tiled=True)  48.4 us
    all_to_all x1, waiting for transfers between devices, body(): lax.all_to_all(sent_rows, 'grp', split_axis=0, concat_axis=0, tiled=True)  33.6 us
    dot_general x1, matrix products, body(): lax.dot_general(grad_up_act, up_weight, contract_units, preferred_element...  12.5 us
    dot_general x1, matrix products, body(): lax.dot_general(grad_gate_act, gate_weight, contract_units, preferred_ele...  11.1 us
  transfers between devices with their start and end apart: 8, of which 6 were waited for; matrix products, arithmetic and copies ran while one was open for 21% of the time, Pallas kernels for 0%

commit v1 on v0

v1 whole, which is shorter than its diff:
```python
import functools

import jax
import jax.numpy as jnp
from jax import lax
from jax.experimental import pallas as pl
from jax.experimental.pallas import tpu as pltpu
from jax.sharding import PartitionSpec as P

MESH = pl.DeviceIdType.MESH
BF = jnp.bfloat16
F32 = jnp.float32
CHUNKS = 4
ROWS_TOP = (((0,), (0,)), ((), ()))
ROWS_BOTH = (((1,), (1,)), ((), ()))


def kernel(cap, f, h, names,
           meta, tok, gout, wg, wu, wd,
           lo, gt, gg, gu, gd,
           picks, sent, tbuf, gbuf, wgu, wdn, act_mine, act_theirs, hid, gact, pout, pback,
           ax1, ax2, az, ay, by, bx1, bx2, bz, home, gwt, gdt, ss, rs, ls):
    d2 = 8 * f
    grp, col = lax.axis_index("grp"), lax.axis_index("col")
    yl, z = grp // 4, grp % 4
    zh, zl = z // 2, z % 2
    yh, x, c = col // 8, (col // 2) % 4, col % 2
    xr, xl, xo = (x + 1) % 4, (x + 3) % 4, (x + 2) % 4

    def dev(yl=yl, z=z, yh=yh, x=x, c=c):
        return (yl * 4 + z, (yh * 4 + x) * 2 + c)

    right, left = dev(x=xr), dev(x=xl)
    other_y, other_z, other_c = dev(yh=1 - yh), dev(z=z + 1 - 2 * zl), dev(c=1 - c)

    def source(k):
        dy, dz = k // 2, k % 2
        return dict(yl=1 - yl if dy else yl, z=3 - z if dz else z)

    counter = [0]
    started = []

    def send(src, dst, target):
        i = counter[0]
        counter[0] += 1
        copy = pltpu.make_async_remote_copy(
            src_ref=src, dst_ref=dst, send_sem=ss.at[i], recv_sem=rs.at[i],
            device_id=target, device_id_type=MESH)
        copy.start()
        started.append(copy)
        return copy

    def got(copies):
        for copy in copies:
            copy.wait_recv()

    def lanes(off, n):
        return pl.ds(pl.multiple_of(off, 128), n)

    def rws(off, n):
        return pl.ds(pl.multiple_of(off, 16), n)

    def off_a(x, yh):
        return (x * 2 + yh) * f

    def off_b(yh, x):
        return (yh * 4 + x) * f

    def add_into(dst, row, n, off, width, *srcs):
        @pl.loop(0, n // 16)
        def _(i):
            at = (rws(row + i * 16, 16), lanes(off, width))
            total = dst[at].astype(F32)
            for src in srcs:
                total = total + src[rws(i * 16, 16), :].astype(F32)
            dst[at] = total.astype(BF)

    barrier = pltpu.get_barrier_semaphore()
    partners = [right, left, other_y, other_z, other_c] + [dev(**source(k)) for k in (1, 2, 3)]
    for partner in partners:
        pl.semaphore_signal(barrier, inc=1, device_id=partner, device_id_type=MESH)
    pl.semaphore_wait(barrier, len(partners))

    for y in range(2):
        for q, w in enumerate((wg, wu)):
            at = (slice(None), y, slice(None), lanes(2 * h * q + h * c, h))
            pltpu.make_async_copy(w.at[y, :, c], wgu.at[at], ls.at[0]).start()
            pltpu.make_async_remote_copy(
                src_ref=w.at[y, :, 1 - c], dst_ref=wgu.at[at], send_sem=ls.at[1], recv_sem=ls.at[2],
                device_id=other_c, device_id_type=MESH).start()
    for p in range(8):
        at = (rws(h * c, h), pl.ds(p * f, f))
        pltpu.make_async_copy(wd.at[:, lanes((p * 2 + c) * f, f)], wdn.at[at], ls.at[3]).start()
        pltpu.make_async_remote_copy(
            src_ref=wd.at[:, lanes((p * 2 + 1 - c) * f, f)], dst_ref=wdn.at[at], send_sem=ls.at[4], recv_sem=ls.at[5],
            device_id=other_c, device_id_type=MESH).start()

    def weights_ready():
        half_gu = wgu.at[:, :, :, pl.ds(0, 2 * h)]
        half_d = wdn.at[pl.ds(0, h)]
        for i, part in ((0, half_gu), (1, half_gu), (2, half_gu), (3, half_d), (4, half_d), (5, half_d)):
            pltpu.make_async_copy(part, part, ls.at[i]).wait()

    first, second = meta[0:1, :], meta[1:2, :]
    share = meta[2:3, :].astype(F32) / 64.0
    count = first.shape[1]
    has, weight = [], []
    for k in range(CHUNKS):
        where = source(k)
        expert = where["yl"] * 2 + where["z"] // 2
        one, two = first == expert, second == expert
        has.append(jnp.logical_or(one, two).astype(F32))
        weight.append(jnp.where(one, share, 1.0 - share))
    marks = jnp.concatenate(has + [jnp.zeros((4, count), F32)], axis=0)
    before = (lax.broadcasted_iota(jnp.int32, (count, count), 0)
              < lax.broadcasted_iota(jnp.int32, (count, count), 1)).astype(F32)
    position = jnp.dot(marks.astype(BF), before.astype(BF), preferred_element_type=F32)
    slot = lax.broadcasted_iota(jnp.int32, (cap, count), 0).astype(F32)
    for k in range(CHUNKS):
        chosen = jnp.where(slot == position[k:k + 1, :], has[k], 0.0)
        picks[0, k] = chosen.astype(BF)
        picks[1, k] = (chosen * weight[k]).astype(BF)
        sent[0, k] = jnp.dot(picks[0, k], tok[...], preferred_element_type=F32).astype(BF)
        sent[1, k] = jnp.dot(picks[1, k], gout[...], preferred_element_type=F32).astype(BF)

    pend = {}
    two = 2 * cap

    def dispatch(k):
        here = (lanes(off_a(x, yh), f), lanes(off_b(yh, x), f))
        if k == 0:
            copies = [pltpu.make_async_copy(sent.at[a, 0], buf.at[rws(zl * cap, cap), here[a]], ls.at[6 + a])
                      for a, buf in enumerate((tbuf, gbuf))]
            for copy in copies:
                copy.start()
            pend["d", k] = copies
            return
        theirs = 1 - zl if k % 2 else zl
        pend["d", k] = [send(sent.at[a, k], buf.at[rws(k * two + theirs * cap, cap), here[a]], dev(**source(k)))
                        for a, buf in enumerate((tbuf, gbuf))]

    def dispatched(k):
        if k == 0:
            for copy in pend["d", 0]:
                copy.wait()
        else:
            got(pend["d", k])

    def put(buf, row, n, off, width, target):
        at = (rws(row, n), lanes(off, width))
        return send(buf.at[at], buf.at[at], target)

    def gather_a(k, phase):
        mine, all_rows = k * two + zl * cap, k * two
        if phase == 1:
            pend["a", k] = [put(tbuf, mine, cap, off_a(x, yh), f, other_y)]
        elif phase == 2:
            got(pend["a", k])
            pend["a", k] = [put(tbuf, mine, cap, off_a(x, 0), 2 * f, other_z)]
        elif phase == 3:
            got(pend["a", k])
            pend["a", k] = [put(tbuf, all_rows, two, off_a(x, 0), 2 * f, right),
                            put(tbuf, all_rows, two, off_a(x, 0), 2 * f, left)]
        elif phase == 4:
            got(pend["a", k])
            pend["a", k] = [put(tbuf, all_rows, cap, off_a(xl, 0), 2 * f, right),
                            put(tbuf, all_rows + cap, cap, off_a(xr, 0), 2 * f, left)]
        else:
            got(pend["a", k])

    def gather_b(k, phase):
        mine, all_rows = k * two + zl * cap, k * two
        if phase == 1:
            pend["b", k] = [put(gbuf, mine, cap, off_b(yh, x), f, other_z)]
        elif phase == 2:
            got(pend["b", k])
            pend["b", k] = [put(gbuf, all_rows, two, off_b(yh, x), f, right),
                            put(gbuf, all_rows, two, off_b(yh, x), f, left)]
        elif phase == 3:
            got(pend["b", k])
            pend["b", k] = [put(gbuf, all_rows, cap, off_b(yh, xl), f, right),
                            put(gbuf, all_rows + cap, cap, off_b(yh, xr), f, left)]
        elif phase == 4:
            got(pend["b", k])
            pend["b", k] = [put(gbuf, all_rows, two, off_b(yh, 0), 4 * f, other_y)]
        else:
            got(pend["b", k])

    def project(k):
        rows = pl.ds(k * two, two)

        @pl.loop(0, 4)
        def _(n):
            w = wgu[:, :, :, lanes(n * h, h)].reshape(d2, h)
            act_mine[rows, lanes(n * h, h)] = jnp.dot(tbuf[rows, :], w, preferred_element_type=F32)

        @pl.loop(0, 2)
        def _(n):
            act_mine[rows, lanes((4 + n) * h, h)] = lax.dot_general(
                gbuf[rows, :], wdn[rws(n * h, h), :], ROWS_BOTH, preferred_element_type=F32)

        pend["p", k] = [send(act_mine.at[rows], act_theirs.at[rows], other_c)]

    def activate(k):
        got(pend["p", k])

        @pl.loop(0, two // 16)
        def _(i):
            rows = rws(k * two + i * 16, 16)
            for n in range(2):
                def both(q):
                    at = (rows, pl.ds((q * 2 + n) * h, h))
                    return act_mine[at] + act_theirs[at]
                gate, up, grad = both(0), both(1), both(2)
                sig = jax.nn.sigmoid(gate)
                silu = gate * sig
                hid[rows, pl.ds(n * h, h)] = (silu * up).astype(BF)
                gact[rows, pl.ds(n * h, h)] = (grad * up * sig * (1.0 + gate * (1.0 - sig))).astype(BF)
                gact[rows, pl.ds((2 + n) * h, h)] = (grad * silu).astype(BF)

    def expand(k):
        rows = pl.ds(k * two, two)

        @pl.loop(0, 4)
        def _(n):
            at = lanes(n * 2 * f, 2 * f)
            pout[rows, at] = jnp.dot(hid[rows, :], wdn[:, at], preferred_element_type=F32).astype(BF)
            w = wgu[n].reshape(2 * f, 4 * h)
            pback[rows, at] = lax.dot_general(
                gact[rows, :], w, ROWS_BOTH, preferred_element_type=F32).astype(BF)

    def reduce_a(k, phase):
        mine, theirs, base = k * two + zl * cap, k * two + (1 - zl) * cap, k * two
        if phase == 1:
            at = lanes(off_a(xo, 0), 2 * f)
            pend["ra", k] = [send(pback.at[rws(base, cap), at], ax1.at[k, 0], right),
                             send(pback.at[rws(base + cap, cap), at], ax1.at[k, 1], left)]
        elif phase == 2:
            got(pend["ra", k])
            add_into(pback, base, cap, off_a(xr, 0), 2 * f, ax1.at[k, 0])
            add_into(pback, base + cap, cap, off_a(xl, 0), 2 * f, ax1.at[k, 1])
            pend["ra", k] = [send(pback.at[rws(base, two), lanes(off_a(xr, 0), 2 * f)], ax2.at[k, 0], right),
                             send(pback.at[rws(base, two), lanes(off_a(xl, 0), 2 * f)], ax2.at[k, 1], left)]
        elif phase == 3:
            got(pend["ra", k])
            add_into(pback, base, two, off_a(x, 0), 2 * f, ax2.at[k, 0], ax2.at[k, 1])
            pend["ra", k] = [send(pback.at[rws(theirs, cap), lanes(off_a(x, 0), 2 * f)], az.at[k], other_z)]
        elif phase == 4:
            got(pend["ra", k])
            add_into(pback, mine, cap, off_a(x, 0), 2 * f, az.at[k])
            pend["ra", k] = [send(pback.at[rws(mine, cap), lanes(off_a(x, 1 - yh), f)], ay.at[k], other_y)]
        else:
            got(pend["ra", k])
            add_into(pback, mine, cap, off_a(x, yh), f, ay.at[k])
            return_home(k, 1, pback, off_a(x, yh))

    def reduce_b(k, phase):
        mine, theirs, base = k * two + zl * cap, k * two + (1 - zl) * cap, k * two
        if phase == 1:
            pend["rb", k] = [send(pout.at[rws(base, two), lanes(off_b(1 - yh, 0), 4 * f)], by.at[k], other_y)]
        elif phase == 2:
            got(pend["rb", k])
            add_into(pout, base, two, off_b(yh, 0), 4 * f, by.at[k])
            at = lanes(off_b(yh, xo), f)
            pend["rb", k] = [send(pout.at[rws(base, cap), at], bx1.at[k, 0], right),
                             send(pout.at[rws(base + cap, cap), at], bx1.at[k, 1], left)]
        elif phase == 3:
            got(pend["rb", k])
            add_into(pout, base, cap, off_b(yh, xr), f, bx1.at[k, 0])
            add_into(pout, base + cap, cap, off_b(yh, xl), f, bx1.at[k, 1])
            pend["rb", k] = [send(pout.at[rws(base, two), lanes(off_b(yh, xr), f)], bx2.at[k, 0], right),
                             send(pout.at[rws(base, two), lanes(off_b(yh, xl), f)], bx2.at[k, 1], left)]
        elif phase == 4:
            got(pend["rb", k])
            add_into(pout, base, two, off_b(yh, x), f, bx2.at[k, 0], bx2.at[k, 1])
            pend["rb", k] = [send(pout.at[rws(theirs, cap), lanes(off_b(yh, x), f)], bz.at[k], other_z)]
        else:
            got(pend["rb", k])
            add_into(pout, mine, cap, off_b(yh, x), f, bz.at[k])
            return_home(k, 0, pout, off_b(yh, x))

    def return_home(k, a, buf, off):
        src = buf.at[rws(k * two + zl * cap, cap), lanes(off, f)]
        if k == 0:
            copy = pltpu.make_async_copy(src, home.at[a, 0], ls.at[8 + a])
            copy.start()
        else:
            copy = send(src, home.at[a, k], dev(**source(k)))
        pend["h", k, a] = copy

    def weight_grads():
        @pl.loop(0, 8)
        def _(p):
            xx, yy = p // 2, p % 2
            gwt[xx, yy] = lax.dot_general(
                tbuf[:, lanes(p * f, f)], gact[...], ROWS_TOP, preferred_element_type=F32).astype(BF)
            for q, out in enumerate((gg, gu)):
                pltpu.make_async_copy(
                    gwt.at[xx, yy, :, lanes(2 * h * q + h * c, h)], out.at[yy, xx, c], ls.at[10]).start()
                pltpu.make_async_remote_copy(
                    src_ref=gwt.at[xx, yy, :, lanes(2 * h * q + h * (1 - c), h)], dst_ref=out.at[yy, xx, c],
                    send_sem=ls.at[11], recv_sem=ls.at[12], device_id=other_c, device_id_type=MESH).start()

        @pl.loop(0, 8)
        def _(p):
            at = lanes(p * f, f)
            gdt[:, at] = lax.dot_general(
                hid[...], gbuf[:, at], ROWS_TOP, preferred_element_type=F32).astype(BF)
            there = lanes((p * 2 + c) * f, f)
            pltpu.make_async_copy(gdt.at[rws(h * c, h), at], gd.at[:, there], ls.at[13]).start()
            pltpu.make_async_remote_copy(
                src_ref=gdt.at[rws(h * (1 - c), h), at], dst_ref=gd.at[:, there],
                send_sem=ls.at[14], recv_sem=ls.at[15], device_id=other_c, device_id_type=MESH).start()

    def weight_grads_done():
        half_gu = gwt.at[:, :, :, pl.ds(0, 2 * h)]
        half_d = gdt.at[pl.ds(0, h)]
        for i, part in ((10, half_gu), (11, half_gu), (12, half_gu), (13, half_d), (14, half_d), (15, half_d)):
            pltpu.make_async_copy(part, part, ls.at[i]).wait()

    def gather(k, phase):
        gather_a(k, phase)
        gather_b(k, phase)

    for k in range(CHUNKS):
        dispatch(k)
    for k in range(CHUNKS):
        dispatched(k)
        gather(k, 1)
    gather(0, 2)
    gather(1, 2)
    gather(0, 3)
    gather(0, 4)
    gather(1, 3)
    gather(2, 2)
    weights_ready()
    for k in range(CHUNKS):
        gather(k, 5)
        if k + 1 < CHUNKS:
            gather(k + 1, 4)
        if k + 2 < CHUNKS:
            gather(k + 2, 3)
        if k + 3 < CHUNKS:
            gather(k + 3, 2)
        project(k)
        if k:
            reduce_a(k - 1, 2)
        activate(k)
        expand(k)
        reduce_a(k, 1)
        reduce_b(k, 1)
        if k:
            reduce_a(k - 1, 3)
            reduce_b(k - 1, 2)
    reduce_a(2, 4)
    reduce_b(2, 3)
    for k in (0, 1):
        reduce_a(k, 4)
        reduce_b(k, 3)
    reduce_a(3, 2)
    weight_grads()
    for k in (0, 1, 2):
        reduce_a(k, 5)
        reduce_b(k, 4)
    reduce_a(3, 3)
    reduce_b(3, 2)
    for k in (0, 1, 2):
        reduce_b(k, 5)
    reduce_a(3, 4)
    reduce_b(3, 3)
    reduce_a(3, 5)
    reduce_b(3, 4)
    reduce_b(3, 5)
    weight_grads_done()
    for a, out in ((1, gt), (0, lo)):
        total = jnp.zeros(out.shape, F32)
        for k in range(CHUNKS):
            if k == 0:
                pend["h", k, a].wait()
            else:
                pend["h", k, a].wait_recv()
            total = total + lax.dot_general(picks[1 - a, k], home[a, k], ROWS_TOP, preferred_element_type=F32)
        out[...] = total.astype(BF)
    for copy in started:
        copy.wait_send()


def body(tokens, grad_out, expert_ids, gate_num, gate_weight, up_weight, down_weight):
    count, f = tokens.shape
    d, h = gate_weight.shape
    cap = 5 * count // 8
    rows, d2 = 8 * cap, 8 * f
    meta = jnp.concatenate([expert_ids.T, gate_num[None, :], jnp.zeros((5, count), jnp.int32)], axis=0)
    split = (2, 4, 2, f, h)
    vm = pl.BlockSpec(memory_space=pltpu.VMEM)
    anywhere = pl.BlockSpec(memory_space=pl.ANY)

    def v(*shape, dtype=BF):
        return pltpu.VMEM(shape, dtype)

    sems = 112
    lo, gt, gg, gu, gd = pl.pallas_call(
        functools.partial(kernel, cap, f, h, None),
        out_shape=(
            jax.ShapeDtypeStruct((count, f), BF), jax.ShapeDtypeStruct((count, f), BF),
            jax.ShapeDtypeStruct(split, BF), jax.ShapeDtypeStruct(split, BF),
            jax.ShapeDtypeStruct((h, d), BF)),
        in_specs=[vm, vm, vm, anywhere, anywhere, anywhere],
        out_specs=(vm, vm, anywhere, anywhere, anywhere),
        scratch_shapes=[
            v(2, 4, cap, count), v(2, 4, cap, f), v(rows, d2), v(rows, d2),
            v(4, 2, f, 4 * h), v(2 * h, d2),
            v(rows, 6 * h, dtype=F32), v(rows, 6 * h, dtype=F32), v(rows, 2 * h), v(rows, 4 * h),
            v(rows, d2), v(rows, d2),
            v(4, 2, cap, 2 * f), v(4, 2, 2 * cap, 2 * f), v(4, cap, 2 * f), v(4, cap, f),
            v(4, 2 * cap, 4 * f), v(4, 2, cap, f), v(4, 2, 2 * cap, f), v(4, cap, f),
            v(2, 4, cap, f), v(4, 2, f, 4 * h), v(2 * h, d2),
            pltpu.SemaphoreType.DMA((sems,)), pltpu.SemaphoreType.DMA((sems,)), pltpu.SemaphoreType.DMA((16,)),
        ],
        compiler_params=pltpu.CompilerParams(
            collective_id=1, has_side_effects=True, vmem_limit_bytes=60 * 2**20),
        name="moe_layer",
    )(meta, tokens, grad_out, gate_weight.reshape(split), up_weight.reshape(split), down_weight)
    return lo, gt, gg.reshape(d, h), gu.reshape(d, h), gd


def solution(mesh):
    placed = (
        P("grp", "col"),
        P("grp", "col"),
        P("grp", None),
        P("grp"),
        P(None, ("grp", "col")),
        P(None, ("grp", "col")),
        P(("grp", "col"), None),
    )
    return jax.shard_map(
        body,
        mesh=mesh,
        in_specs=placed,
        out_specs=(
            P("grp", "col"),
            P("grp", "col"),
            P(None, ("grp", "col")),
            P(None, ("grp", "col")),
            P(("grp", "col"), None),
        ),
        check_vma=False,
    )
```

time: 546 us -> 161 us (0.29)
  waiting for transfers between devices: 322 us -> 0 us
  Pallas kernels: 0 us -> 147 us
  local copies, waits for them, and re-layouts: 97 us -> 11.8 us
  matrix products: 79.3 us -> 0 us
  starting transfers between devices: 19.4 us -> 0 us
  between operations: 14 us -> 0.65 us
  other arithmetic: 11.6 us -> 1.36 us
    pallas_call x0 -> x1, Pallas kernels: none -> 147 us  [body(): pl.pallas_call(functools.partial(kernel, cap, f, h, None), out_shape=(jax...]
    unnamed x6 -> x0, waiting for transfers between devices: 113 us -> none
    all_to_all x4 -> x0, waiting for transfers between devices: 108 us -> none  [the longest x1 74 us: body(): lax.all_to_all(sent_grads, 'grp', split_axis=0, concat_axis=0, tiled=True)]
    all_gather x2 -> x0, waiting for transfers between devices: 102 us -> none  [the longest x1 53.3 us: body(): lax.all_gather(grad_out, 'col', axis=1, tiled=True)]
    dot_general x11 -> x0, matrix products: 79.3 us -> none  [the longest x1 12.5 us: body(): lax.dot_general(grad_up_act, up_weight, contract_units, preferred_element...]
    unnamed x27 -> x9, local copies, waits for them, and re-layouts: 77.3 us -> 11.7 us
    all_to_all x4 -> x0, starting transfers between devices: 18.9 us -> none  [the longest x1 5.07 us: body(): lax.all_to_all(sent_rows, 'grp', split_axis=0, concat_axis=0, tiled=True)]
    broadcast_in_dim x3 -> x1, local copies, waits for them, and re-layouts: 10.5 us -> 0.01 us  [body(): jnp.zeros((5, count), jnp.int32)]
  transfers between devices with their start and end apart: 8 -> 0, of which waited for: 6 -> 0; matrix products, arithmetic and copies ran while one was open for 21% -> 0% of each run, Pallas kernels for 0% -> 0%
where the time goes in v1:
time: 161 us
  Pallas kernels  147 us (91%)
  local copies, waits for them, and re-layouts  11.8 us (7%)
    pallas_call x1, Pallas kernels, body(): pl.pallas_call(functools.partial(kernel, cap, f, h, None), out_shape=(jax...  147 us
    unnamed x9, local copies, waits for them, and re-layouts  11.7 us

profile of v1, /device:TPU:0, one launch (start us, length us, event | category | flops | bytes accessed | tf_op | source)
XLA Modules:
  0.0 160.6 jit_solution(1056304042853288686)
XLA Ops:
  0.6 0.1 pad.2.clone
  0.7 1.4 add_add_fusion.meta
  2.1 146.8 %moe_layer.1 = (bf16[128,384]{1,0:T(8,128)(2,1)}, bf16[128,384]{1,0:T(8,128)(2,1)}, bf16[2,4,2,384,256]{4,3,2,1,0:T(8,128)(2,1)}, bf16[2,4,2,384,256]{4,3,2,1,0:T(8,128)(2,1)}, bf16[256,6144]{1,0:T(8,128)(2,1)}) custom-call(s32[8,128]{1,0:T(8,128)} %add_add_fusion.meta, bf16[128,384]{1,0:T(8,128)(2,1)} %tok.1, bf16[128,384]{1,0:T(8,128)(2,1)} %gout.1, ...), custom_call_target="tpu_custom_call" | custom-call | tf_op jit(solution)/shard_map/moe_layer/pallas_call | solution.py:402
  148.9 1.5 copy.17
  150.4 1.5 copy.18
  152.0 0.0 copy-start.1
  152.0 3.9 %copy.19 = bf16[6144,256]{1,0:T(8,128)(2,1)} copy(bf16[6144,256]{1,0:T(8,128)(2,1)} %bitcast.7) | data formatting | bytes 6291456
  155.9 0.0 copy-done.1
  155.9 0.0 copy-start
  155.9 1.7 %copy.20 = bf16[6144,256]{1,0:T(8,128)(2,1)} copy(bf16[6144,256]{1,0:T(8,128)(2,1)S(1)} %bitcast.6) | data formatting | bytes 6291456
  157.6 1.4 copy-done
  158.9 1.7 %copy.21 = bf16[256,6144]{1,0:T(8,128)(2,1)} copy(bf16[256,6144]{1,0:T(8,128)(2,1)S(1)} %copy-done) | data formatting | bytes 6291456
  (1 shorter events, 0.0 us)
Async XLA Ops:
  152.0 3.9 %copy-start.1 = (bf16[2,4,2,384,256]{4,3,2,1,0:T(8,128)(2,1)S(1)}, bf16[2,4,2,384,256]{4,3,2,1,0:T(8,128)(2,1)}, u32[]{:S(2)}) copy-start(bf16[2,4,2,384,256]{4,3,2,1,0:T(8,128)(2,1)} %get-tuple-element.13) | copy-start | bytes 9437188
  155.9 3.0 %copy-start = (bf16[256,6144]{1,0:T(8,128)(2,1)S(1)}, bf16[256,6144]{1,0:T(8,128)(2,1)}, u32[]{:S(2)}) copy-start(bf16[256,6144]{1,0:T(8,128)(2,1)} %get-tuple-element.24) | copy-start | bytes 9437188

commit v2 on v1

v2 whole, which is shorter than its diff:
```python
import functools

import jax
import jax.numpy as jnp
from jax import lax
from jax.experimental import pallas as pl
from jax.experimental.pallas import tpu as pltpu
from jax.sharding import PartitionSpec as P

MESH = pl.DeviceIdType.MESH
BF = jnp.bfloat16
F32 = jnp.float32
CHUNKS = 4
ROWS_TOP = (((0,), (0,)), ((), ()))
ROWS_BOTH = (((1,), (1,)), ((), ()))
GATHER = (("zyx", "zyx", "yzx", "yzx"), ("xzy", "xyz", "xzy", "xyz"))
REDUCE = (("xzy", "xyz", "xzy", "zxy"), ("yzx", "yzx", "yxz", "zyx"))
ORDER = (
    "d11", "d21", "d31", "d20", "d10", "d00", "d30", "d01", "g001", "g011", "g111", "g211", "g002", "g101",
    "g012", "g311", "g112", "g201", "g102", "g212", "g301", "g013", "g003", "g312", "g202", "g113", "g213", "g103",
    "g302", "g014", "g004", "g313", "g203", "g114", "g104", "g214", "t0", "g303", "p0", "s0", "g204", "t1",
    "g314", "v0", "o0", "r001", "p1", "g304", "s1", "b0", "t2", "v1", "o1", "r101", "t3", "p2",
    "s2", "p3", "s3", "r011", "b1", "r111", "v2", "o2", "r201", "b2", "r211", "r112", "v3", "o3",
    "r301", "r102", "b3", "r311", "r002", "r012", "n0", "r113", "w0", "w2", "r312", "r202", "w1", "r212",
    "w3", "r013", "n2", "n1", "r003", "n3", "r114", "r313", "r302", "r213", "r004", "r303", "r203", "r103",
    "r214", "h11", "r014", "h00", "r314", "r304", "r204", "h21", "r104", "h01", "h31", "h30", "h20", "h10",
)


def boxes(cap, f):
    found = []
    for k in range(CHUNKS):
        for a in range(2):
            phase = 0
            for i in (2, 1, 0):
                axis, axes = REDUCE[a][k][i], REDUCE[a][k][:i]
                n = 2 * cap if "z" in axes else cap
                width = f * (4 if "x" in axes else 1) * (2 if "y" in axes else 1)
                phase += 1
                if axis == "x":
                    top = -(-n // 32) * 16
                    found += [((k, a, phase), (top, width)), ((k, a, phase), (n - top, width))]
                    phase += 1
                    found += [((k, a, phase), (n, width))] * 2
                else:
                    found.append(((k, a, phase), (n, width)))
    return found


def box_keys():
    return [key for key, _ in boxes(16, 128)]


def kernel(cap, f, h,
           meta, tok, gout, wg, wu, wd,
           lo, gt, gg, gu, gd,
           picks, sent, tbuf, gbuf, wgu, wdn, act_mine, act_theirs, hid, gact, pout, pback,
           home, gwt, gdt, ss, rs, ls, *landings):
    d2 = 8 * f
    grp, col = lax.axis_index("grp"), lax.axis_index("col")
    yl, z = grp // 4, grp % 4
    zh, zl = z // 2, z % 2
    yh, x, c = col // 8, (col // 2) % 4, col % 2
    xr, xl, xo = (x + 1) % 4, (x + 3) % 4, (x + 2) % 4

    def dev(yl=yl, z=z, yh=yh, x=x, c=c):
        return (yl * 4 + z, (yh * 4 + x) * 2 + c)

    right, left = dev(x=xr), dev(x=xl)
    other_y, other_z, other_c = dev(yh=1 - yh), dev(z=z + 1 - 2 * zl), dev(c=1 - c)

    def source(k):
        dy, dz = k // 2, k % 2
        return dict(yl=1 - yl if dy else yl, z=3 - z if dz else z)

    counter = [0]
    started = []
    inbox, landing = {}, {}
    for key, box in zip(box_keys(), landings):
        inbox.setdefault(key, []).append(box)

    def send(src, dst, target):
        i = counter[0]
        counter[0] += 1
        copy = pltpu.make_async_remote_copy(
            src_ref=src, dst_ref=dst, send_sem=ss.at[i], recv_sem=rs.at[i],
            device_id=target, device_id_type=MESH)
        copy.start()
        started.append(copy)
        return copy

    def got(copies):
        for copy in copies:
            copy.wait_recv()

    def lanes(off, n):
        return pl.ds(pl.multiple_of(off, 128), n)

    def rws(off, n):
        return pl.ds(pl.multiple_of(off, 16), n)

    def off_a(x, yh):
        return (x * 2 + yh) * f

    def off_b(yh, x):
        return (yh * 4 + x) * f

    def add_into(dst, row, n, off, width, *srcs):
        @pl.loop(0, n // 16)
        def _(i):
            at = (rws(row + i * 16, 16), lanes(off, width))
            total = dst[at].astype(F32)
            for src in srcs:
                total = total + src[rws(i * 16, 16), :].astype(F32)
            dst[at] = total.astype(BF)

    barrier = pltpu.get_barrier_semaphore()
    partners = [right, left, other_y, other_z, other_c] + [dev(**source(k)) for k in (1, 2, 3)]
    for partner in partners:
        pl.semaphore_signal(barrier, inc=1, device_id=partner, device_id_type=MESH)

    for y in range(2):
        for q, w in enumerate((wg, wu)):
            at = (slice(None), y, slice(None), lanes(2 * h * q + h * c, h))
            pltpu.make_async_copy(w.at[y, :, c], wgu.at[at], ls.at[0]).start()
    for p in range(8):
        at = (rws(h * c, h), pl.ds(p * f, f))
        pltpu.make_async_copy(wd.at[:, lanes((p * 2 + c) * f, f)], wdn.at[at], ls.at[3]).start()

    def weights_from_other():
        for y in range(2):
            for q, w in enumerate((wg, wu)):
                at = (slice(None), y, slice(None), lanes(2 * h * q + h * c, h))
                pltpu.make_async_remote_copy(
                    src_ref=w.at[y, :, 1 - c], dst_ref=wgu.at[at], send_sem=ls.at[1], recv_sem=ls.at[2],
                    device_id=other_c, device_id_type=MESH).start()
        for p in range(8):
            at = (rws(h * c, h), pl.ds(p * f, f))
            pltpu.make_async_remote_copy(
                src_ref=wd.at[:, lanes((p * 2 + 1 - c) * f, f)], dst_ref=wdn.at[at], send_sem=ls.at[4],
                recv_sem=ls.at[5], device_id=other_c, device_id_type=MESH).start()

    ready = []

    def weights_ready():
        half_gu = wgu.at[:, :, :, pl.ds(0, 2 * h)]
        half_d = wdn.at[pl.ds(0, h)]
        for i, part in ((0, half_gu), (1, half_gu), (2, half_gu), (3, half_d), (4, half_d), (5, half_d)):
            pltpu.make_async_copy(part, part, ls.at[i]).wait()

    first, second = meta[0:1, :], meta[1:2, :]
    share = meta[2:3, :].astype(F32) / 64.0
    count = first.shape[1]
    has, weight = [], []
    for k in range(CHUNKS):
        where = source(k)
        expert = where["yl"] * 2 + where["z"] // 2
        one, two = first == expert, second == expert
        has.append(jnp.logical_or(one, two).astype(F32))
        weight.append(jnp.where(one, share, 1.0 - share))
    marks = jnp.concatenate(has + [jnp.zeros((4, count), F32)], axis=0)
    before = (lax.broadcasted_iota(jnp.int32, (count, count), 0)
              < lax.broadcasted_iota(jnp.int32, (count, count), 1)).astype(F32)
    position = jnp.dot(marks.astype(BF), before.astype(BF), preferred_element_type=F32)
    slot = lax.broadcasted_iota(jnp.int32, (cap, count), 0).astype(F32)
    for k in range(CHUNKS):
        chosen = jnp.where(slot == position[k:k + 1, :], has[k], 0.0)
        picks[0, k] = chosen.astype(BF)
        picks[1, k] = (chosen * weight[k]).astype(BF)
        sent[0, k] = jnp.dot(picks[0, k], tok[...], preferred_element_type=F32).astype(BF)
        sent[1, k] = jnp.dot(picks[1, k], gout[...], preferred_element_type=F32).astype(BF)

    pend = {}
    two = 2 * cap
    bufs = (tbuf, gbuf)
    sums = (pout, pback)

    def region(tokens_first, k, axes, z=zl, x=x, y=yh):
        row, n = (k * two, two) if "z" in axes else (k * two + z * cap, cap)
        if "x" in axes and "y" in axes:
            off, width = 0, d2
        elif tokens_first:
            off, width = (off_a(x, 0), 2 * f) if "y" in axes else (off_a(x, y), f)
        else:
            off, width = (off_b(y, 0), 4 * f) if "x" in axes else (off_b(y, x), f)
        return row, n, off, width

    def view(buf, part):
        row, n, off, width = part
        return buf.at[rws(row, n), lanes(off, width)]

    def halves(part):
        row, n, off, width = part
        top = -(-n // 32) * 16
        return (row, top, off, width), (row + top, n - top, off, width)

    def dispatch(k, a):
        off = (off_a(x, yh), off_b(yh, x))[a]
        theirs = 1 - zl if k % 2 else zl
        dst = bufs[a].at[rws(k * two + theirs * cap, cap), lanes(off, f)]
        if k == 0:
            copy = pltpu.make_async_copy(sent.at[a, 0], dst, ls.at[6 + a])
            copy.start()
            pend["g", k, a] = [copy]
        else:
            pend["g", k, a] = [send(sent.at[a, k], dst, dev(**source(k)))]

    def gathered(k, a, phase):
        if phase == 0 and k == 0:
            pend["g", k, a][0].wait()
        else:
            got(pend["g", k, a])

    def gather(k, a, phase):
        gathered(k, a, phase - 1)
        steps = []
        for i, axis in enumerate(GATHER[a][k]):
            steps += [(axis, i, 0), (axis, i, 1)] if axis == "x" else [(axis, i, 0)]
        axis, i, later = steps[phase - 1]
        buf, axes = bufs[a], GATHER[a][k][:i]
        if axis == "x" and later:
            up = view(buf, halves(region(a == 0, k, axes, x=xl))[0])
            down = view(buf, halves(region(a == 0, k, axes, x=xr))[1])
            pend["g", k, a] = [send(up, up, right), send(down, down, left)]
        else:
            mine = view(buf, region(a == 0, k, axes))
            to = (right, left) if axis == "x" else (other_y,) if axis == "y" else (other_z,)
            pend["g", k, a] = [send(mine, mine, target) for target in to]

    def project_tokens(k):
        gathered(k, 0, 4)
        rows = pl.ds(k * two, two)
        if not ready:
            weights_ready()
            ready.append(True)

        @pl.loop(0, 2)
        def _(n):
            w = wgu[:, :, :, lanes(n * 2 * h, 2 * h)].reshape(d2, 2 * h)
            act_mine[rows, lanes(n * 2 * h, 2 * h)] = jnp.dot(tbuf[rows, :], w, preferred_element_type=F32)

    def project_grads(k):
        gathered(k, 1, 4)
        rows = pl.ds(k * two, two)
        if not ready:
            weights_ready()
            ready.append(True)

        @pl.loop(0, 2)
        def _(n):
            act_mine[rows, lanes((4 + n) * h, h)] = lax.dot_general(
                gbuf[rows, :], wdn[rws(n * h, h), :], ROWS_BOTH, preferred_element_type=F32)

    def swap(k):
        rows = pl.ds(k * two, two)
        pend["p", k] = [send(act_mine.at[rows], act_theirs.at[rows], other_c)]

    def activate(k):
        got(pend["p", k])

        @pl.loop(0, two // 16)
        def _(i):
            rows = rws(k * two + i * 16, 16)
            for n in range(2):
                def both(q):
                    at = (rows, pl.ds((q * 2 + n) * h, h))
                    return act_mine[at] + act_theirs[at]
                gate, up, grad = both(0), both(1), both(2)
                sig = jax.nn.sigmoid(gate)
                silu = gate * sig
                hid[rows, pl.ds(n * h, h)] = (silu * up).astype(BF)
                gact[rows, pl.ds(n * h, h)] = (grad * up * sig * (1.0 + gate * (1.0 - sig))).astype(BF)
                gact[rows, pl.ds((2 + n) * h, h)] = (grad * silu).astype(BF)

    def expand_out(k):
        rows = pl.ds(k * two, two)

        @pl.loop(0, 4)
        def _(n):
            at = lanes(n * 2 * f, 2 * f)
            pout[rows, at] = jnp.dot(hid[rows, :], wdn[:, at], preferred_element_type=F32).astype(BF)

    def expand_back(k):
        rows = pl.ds(k * two, two)

        @pl.loop(0, 4)
        def _(n):
            w = wgu[n].reshape(2 * f, 4 * h)
            pback[rows, lanes(n * 2 * f, 2 * f)] = lax.dot_general(
                gact[rows, :], w, ROWS_BOTH, preferred_element_type=F32).astype(BF)

    def swap_in(k, a, landed):
        got(pend["r", k, a])
        for part, slots in landed:
            row, n, off, width = part
            add_into(sums[a], row, n, off, width, *slots)

    def reduce(k, a, phase):
        steps = []
        for i in (2, 1, 0):
            axis = REDUCE[a][k][i]
            steps += [(axis, i, 0), (axis, i, 1)] if axis == "x" else [(axis, i, 0)]
        if phase > 1:
            swap_in(k, a, landing[k, a])
        axis, i, later = steps[phase - 1]
        first_x, axes = a == 1, REDUCE[a][k][:i]
        place = functools.partial(region, first_x, k, axes)
        if axis == "x":
            up, down = place(x=xr if later else xo), place(x=xl if later else xo)
            if not later:
                up, down = halves(up)[0], halves(down)[1]
            moves = [(up, right), (down, left)]
            if later:
                added = [(place(), (0, 1))]
            else:
                added = [(halves(place(x=xr))[0], (0,)), (halves(place(x=xl))[1], (1,))]
        elif axis == "y":
            moves, added = [(place(y=1 - yh), other_y)], [(place(), (0,))]
        else:
            moves, added = [(place(z=1 - zl), other_z)], [(place(), (0,))]
        slots = inbox[k, a, phase]
        pend["r", k, a] = [send(view(sums[a], part), slot, target) for (part, target), slot in zip(moves, slots)]
        landing[k, a] = [(part, [slots[j] for j in which]) for part, which in added]

    def return_home(k, a):
        swap_in(k, a, landing[k, a])
        src = view(sums[a], region(a == 1, k, ""))
        if k == 0:
            copy = pltpu.make_async_copy(src, home.at[a, 0], ls.at[8 + a])
            copy.start()
        else:
            copy = send(src, home.at[a, k], dev(**source(k)))
        pend["h", k, a] = copy

    def weight_grads_up(part):
        @pl.loop(part * 2, part * 2 + 2)
        def _(p):
            xx, yy = p // 2, p % 2
            gwt[xx, yy] = lax.dot_general(
                tbuf[:, lanes(p * f, f)], gact[...], ROWS_TOP, preferred_element_type=F32).astype(BF)
            for q, out in enumerate((gg, gu)):
                pltpu.make_async_copy(
                    gwt.at[xx, yy, :, lanes(2 * h * q + h * c, h)], out.at[yy, xx, c], ls.at[10]).start()
                pltpu.make_async_remote_copy(
                    src_ref=gwt.at[xx, yy, :, lanes(2 * h * q + h * (1 - c), h)], dst_ref=out.at[yy, xx, c],
                    send_sem=ls.at[11], recv_sem=ls.at[12], device_id=other_c, device_id_type=MESH).start()

    def weight_grads_down(part):
        @pl.loop(part * 2, part * 2 + 2)
        def _(p):
            at = lanes(p * f, f)
            gdt[:, at] = lax.dot_general(
                hid[...], gbuf[:, at], ROWS_TOP, preferred_element_type=F32).astype(BF)
            there = lanes((p * 2 + c) * f, f)
            pltpu.make_async_copy(gdt.at[rws(h * c, h), at], gd.at[:, there], ls.at[13]).start()
            pltpu.make_async_remote_copy(
                src_ref=gdt.at[rws(h * (1 - c), h), at], dst_ref=gd.at[:, there],
                send_sem=ls.at[14], recv_sem=ls.at[15], device_id=other_c, device_id_type=MESH).start()

    def weight_grads_done():
        half_gu = gwt.at[:, :, :, pl.ds(0, 2 * h)]
        half_d = gdt.at[pl.ds(0, h)]
        for i, part in ((10, half_gu), (11, half_gu), (12, half_gu), (13, half_d), (14, half_d), (15, half_d)):
            pltpu.make_async_copy(part, part, ls.at[i]).wait()

    steps = dict(d=dispatch, g=gather, t=project_tokens, p=project_grads, s=swap, v=activate, o=expand_out,
                 b=expand_back, r=reduce, h=return_home, w=weight_grads_up, n=weight_grads_down)
    pl.semaphore_wait(barrier, len(partners))
    weights_from_other()
    for step in ORDER:
        steps[step[0]](*(int(digit) for digit in step[1:]))
    weight_grads_done()
    for a, out in ((1, gt), (0, lo)):
        total = jnp.zeros(out.shape, F32)
        for k in range(CHUNKS):
            if k == 0:
                pend["h", k, a].wait()
            else:
                pend["h", k, a].wait_recv()
            total = total + lax.dot_general(picks[1 - a, k], home[a, k], ROWS_TOP, preferred_element_type=F32)
        out[...] = total.astype(BF)
    for copy in started:
        copy.wait_send()


def body(tokens, grad_out, expert_ids, gate_num, gate_weight, up_weight, down_weight):
    count, f = tokens.shape
    d, h = gate_weight.shape
    cap = 5 * count // 8
    rows, d2 = 8 * cap, 8 * f
    meta = jnp.concatenate([expert_ids.T, gate_num[None, :], jnp.zeros((5, count), jnp.int32)], axis=0)
    split = (2, 4, 2, f, h)
    vm = pl.BlockSpec(memory_space=pltpu.VMEM)
    anywhere = pl.BlockSpec(memory_space=pl.ANY)

    def v(*shape, dtype=BF):
        return pltpu.VMEM(shape, dtype)

    sems = 112
    lo, gt, gg, gu, gd = pl.pallas_call(
        functools.partial(kernel, cap, f, h),
        out_shape=(
            jax.ShapeDtypeStruct((count, f), BF), jax.ShapeDtypeStruct((count, f), BF),
            jax.ShapeDtypeStruct(split, BF), jax.ShapeDtypeStruct(split, BF),
            jax.ShapeDtypeStruct((h, d), BF)),
        in_specs=[vm, vm, vm, anywhere, anywhere, anywhere],
        out_specs=(vm, vm, anywhere, anywhere, anywhere),
        scratch_shapes=[
            v(2, 4, cap, count), v(2, 4, cap, f), v(rows, d2), v(rows, d2),
            v(4, 2, f, 4 * h), v(2 * h, d2),
            v(rows, 6 * h, dtype=F32), v(rows, 6 * h, dtype=F32), v(rows, 2 * h), v(rows, 4 * h),
            v(rows, d2), v(rows, d2),
            v(2, 4, cap, f), v(4, 2, f, 4 * h), v(2 * h, d2),
            pltpu.SemaphoreType.DMA((sems,)), pltpu.SemaphoreType.DMA((sems,)), pltpu.SemaphoreType.DMA((16,)),
        ] + [v(*shape) for _, shape in boxes(cap, f)],
        compiler_params=pltpu.CompilerParams(
            collective_id=1, has_side_effects=True, vmem_limit_bytes=60 * 2**20),
        name="moe_layer",
    )(meta, tokens, grad_out, gate_weight.reshape(split), up_weight.reshape(split), down_weight)
    return lo, gt, gg.reshape(d, h), gu.reshape(d, h), gd


def solution(mesh):
    placed = (
        P("grp", "col"),
        P("grp", "col"),
        P("grp", None),
        P("grp"),
        P(None, ("grp", "col")),
        P(None, ("grp", "col")),
        P(("grp", "col"), None),
    )
    return jax.shard_map(
        body,
        mesh=mesh,
        in_specs=placed,
        out_specs=(
            P("grp", "col"),
            P("grp", "col"),
            P(None, ("grp", "col")),
            P(None, ("grp", "col")),
            P(("grp", "col"), None),
        ),
        check_vma=False,
    )
```

time: 161 us -> 125 us (0.78)
  Pallas kernels: 147 us -> 111 us
    pallas_call x1, Pallas kernels: 147 us -> 111 us  [body(): pl.pallas_call(functools.partial(kernel, cap, f, h), out_shape=(jax.Shape...]
where the time goes in v2:
time: 125 us
  Pallas kernels  111 us (89%)
  local copies, waits for them, and re-layouts  11.8 us (9%)
  other arithmetic  1.36 us (1%)
    pallas_call x1, Pallas kernels, body(): pl.pallas_call(functools.partial(kernel, cap, f, h), out_shape=(jax.Shape...  111 us
    unnamed x9, local copies, waits for them, and re-layouts  11.7 us

profile of v2, /device:TPU:0, one launch (start us, length us, event | category | flops | bytes accessed | tf_op | source)
XLA Modules:
  0.0 125.0 jit_solution(9052185168493990348)
XLA Ops:
  0.6 0.1 pad.2.clone
  0.7 1.4 %add_add_fusion.meta = s32[8,128]{1,0:T(8,128)} fusion(s32[1,128]{1,0:T(1,128)} %bitcast.11, s32[2,128]{1,0:T(2,128)} %bitcast.10, s32[8]{0:T(128)S(1)} %pad.2.clone), kind=kLoop, calls=%fused_computation | loop fusion | flops 2048 | bytes 5664 | tf_op jit(solution)/shard_map/concatenate | solution.py:391
  2.1 111.2 %moe_layer.1 = (bf16[128,384]{1,0:T(8,128)(2,1)}, bf16[128,384]{1,0:T(8,128)(2,1)}, bf16[2,4,2,384,256]{4,3,2,1,0:T(8,128)(2,1)}, bf16[2,4,2,384,256]{4,3,2,1,0:T(8,128)(2,1)}, bf16[256,6144]{1,0:T(8,128)(2,1)}) custom-call(s32[8,128]{1,0:T(8,128)} %add_add_fusion.meta, bf16[128,384]{1,0:T(8,128)(2,1)} %tok.1, bf16[128,384]{1,0:T(8,128)(2,1)} %gout.1, ...), custom_call_target="tpu_custom_call" | custom-call | tf_op jit(solution)/shard_map/moe_layer/pallas_call | solution.py:400
  113.3 1.5 %copy.17 = bf16[128,384]{1,0:T(8,128)(2,1)} copy(bf16[128,384]{1,0:T(8,128)(2,1)} %get-tuple-element.20) | data formatting | bytes 196608
  114.8 1.5 %copy.18 = bf16[128,384]{1,0:T(8,128)(2,1)} copy(bf16[128,384]{1,0:T(8,128)(2,1)} %get-tuple-element.21) | data formatting | bytes 196608
  116.4 0.0 copy-start.1
  116.4 3.9 %copy.19 = bf16[6144,256]{1,0:T(8,128)(2,1)} copy(bf16[6144,256]{1,0:T(8,128)(2,1)} %bitcast.7) | data formatting | bytes 6291456
  120.3 0.0 copy-done.1
  120.3 0.0 copy-start
  120.3 1.7 %copy.20 = bf16[6144,256]{1,0:T(8,128)(2,1)} copy(bf16[6144,256]{1,0:T(8,128)(2,1)S(1)} %bitcast.6) | data formatting | bytes 6291456
  121.9 1.4 %copy-done = bf16[256,6144]{1,0:T(8,128)(2,1)S(1)} copy-done((bf16[256,6144]{1,0:T(8,128)(2,1)S(1)}, bf16[256,6144]{1,0:T(8,128)(2,1)}, u32[]{:S(2)}) %copy-start) | copy-done | bytes 3145752
  123.3 1.7 %copy.21 = bf16[256,6144]{1,0:T(8,128)(2,1)} copy(bf16[256,6144]{1,0:T(8,128)(2,1)S(1)} %copy-done) | data formatting | bytes 6291456
  (1 shorter events, 0.0 us)
Async XLA Ops:
  116.4 3.9 %copy-start.1 = (bf16[2,4,2,384,256]{4,3,2,1,0:T(8,128)(2,1)S(1)}, bf16[2,4,2,384,256]{4,3,2,1,0:T(8,128)(2,1)}, u32[]{:S(2)}) copy-start(bf16[2,4,2,384,256]{4,3,2,1,0:T(8,128)(2,1)} %get-tuple-element.13) | copy-start | bytes 9437188
  120.3 3.0 %copy-start = (bf16[256,6144]{1,0:T(8,128)(2,1)S(1)}, bf16[256,6144]{1,0:T(8,128)(2,1)}, u32[]{:S(2)}) copy-start(bf16[256,6144]{1,0:T(8,128)(2,1)} %get-tuple-element.24) | copy-start | bytes 9437188

commit v3 on v2

--- a/solution.py
+++ b/solution.py
@@ -13,17 +13,17 @@
 CHUNKS = 4
 ROWS_TOP = (((0,), (0,)), ((), ()))
 ROWS_BOTH = (((1,), (1,)), ((), ()))
-GATHER = (("zyx", "zyx", "yzx", "yzx"), ("xzy", "xyz", "xzy", "xyz"))
-REDUCE = (("xzy", "xyz", "xzy", "zxy"), ("yzx", "yzx", "yxz", "zyx"))
+GATHER = (("zyx", "yzx", "zyx", "yzx"), ("xzy", "xyz", "xyz", "xzy"))
+REDUCE = (("zxy", "xzy", "xyz", "xyz"), ("yzx", "zyx", "yzx", "yzx"))
 ORDER = (
-    "d11", "d21", "d31", "d20", "d10", "d00", "d30", "d01", "g001", "g011", "g111", "g211", "g002", "g101",
-    "g012", "g311", "g112", "g201", "g102", "g212", "g301", "g013", "g003", "g312", "g202", "g113", "g213", "g103",
-    "g302", "g014", "g004", "g313", "g203", "g114", "g104", "g214", "t0", "g303", "p0", "s0", "g204", "t1",
-    "g314", "v0", "o0", "r001", "p1", "g304", "s1", "b0", "t2", "v1", "o1", "r101", "t3", "p2",
-    "s2", "p3", "s3", "r011", "b1", "r111", "v2", "o2", "r201", "b2", "r211", "r112", "v3", "o3",
-    "r301", "r102", "b3", "r311", "r002", "r012", "n0", "r113", "w0", "w2", "r312", "r202", "w1", "r212",
-    "w3", "r013", "n2", "n1", "r003", "n3", "r114", "r313", "r302", "r213", "r004", "r303", "r203", "r103",
-    "r214", "h11", "r014", "h00", "r314", "r304", "r204", "h21", "r104", "h01", "h31", "h30", "h20", "h10",
+    "d31", "d00", "d01", "d21", "g001", "d20", "d10", "d11", "g011", "d30", "g311", "g002", "g101", "g211",
+    "g012", "g111", "g201", "g312", "g301", "g212", "g013", "g202", "g003", "g112", "g102", "g313", "g213", "g302",
+    "g203", "g014", "g004", "g113", "g103", "g214", "g204", "g314", "t0", "g303", "p0", "s0", "g104", "t2",
+    "g114", "v0", "b0", "g304", "p2", "r011", "s2", "o0", "t1", "r001", "t3", "v2", "o2", "r201",
+    "r012", "p3", "s3", "p1", "s1", "b2", "r211", "v3", "b3", "r311", "v1", "r013", "o1", "r101",
+    "r212", "o3", "r301", "r202", "b1", "r111", "r312", "r014", "r002", "w0", "r213", "n1", "n2", "r112",
+    "w2", "r102", "n0", "r302", "w3", "r313", "r214", "r003", "n3", "r203", "h01", "w1", "r113", "r103",
+    "r303", "r314", "r004", "r204", "h21", "r104", "r304", "r114", "h00", "h20", "h31", "h10", "h30", "h11",
 )
 
 
@@ -51,16 +51,70 @@
     return [key for key, _ in boxes(16, 128)]
 
 
+def place():
+    grp, col = lax.axis_index("grp"), lax.axis_index("col")
+    return grp // 4, grp % 4, col // 8, (col // 2) % 4, col % 2
+
+
+def sources(yl, z):
+    return [dict(yl=1 - yl if k // 2 else yl, z=3 - z if k % 2 else z) for k in range(CHUNKS)]
+
+
+def routing(cap, ids, nums, yl, z):
+    first, second = ids[0:1, :], ids[1:2, :]
+    share = nums[...].astype(F32) / 64.0
+    count = first.shape[1]
+    has, weight = [], []
+    for where in sources(yl, z):
+        expert = where["yl"] * 2 + where["z"] // 2
+        one, two = first == expert, second == expert
+        has.append(jnp.logical_or(one, two).astype(F32))
+        weight.append(jnp.where(one, share, 1.0 - share))
+    marks = jnp.concatenate(has + [jnp.zeros((4, count), F32)], axis=0)
+    before = (lax.broadcasted_iota(jnp.int32, (count, count), 0)
+              < lax.broadcasted_iota(jnp.int32, (count, count), 1)).astype(F32)
+    position = jnp.dot(marks.astype(BF), before.astype(BF), preferred_element_type=F32)
+    slot = lax.broadcasted_iota(jnp.int32, (cap, count), 0).astype(F32)
+    found = []
+    for k in range(CHUNKS):
+        chosen = jnp.where(slot == position[k:k + 1, :], has[k], 0.0)
+        found.append((chosen.astype(BF), (chosen * weight[k]).astype(BF)))
+    return found
+
+
+def finish(cap, parts, ids, nums, home, gg, gu, gd, lo, gt, ggo, guo, gdo, tall, wide, into, out_of):
+    long, across = gg.shape[0] // parts, gd.shape[1] // parts
+    ins, outs = [], []
+    for i in range(parts):
+        rows, lanes = (pl.ds(i * long, long), slice(None)), (slice(None), pl.ds(i * across, across))
+        for q, (src, held, dst, at) in enumerate((
+                (gg, tall.at[0], ggo, rows), (gu, tall.at[1], guo, rows), (gd, wide, gdo, lanes))):
+            ins.append(pltpu.make_async_copy(src.at[at], held.at[at], into.at[q, i]))
+            outs.append(pltpu.make_async_copy(held.at[at], dst.at[at], out_of.at[q, i]))
+    for copy in ins:
+        copy.start()
+    for landed, leaving in zip(ins, outs):
+        landed.wait()
+        leaving.start()
+    yl, z, _, _, _ = place()
+    picks = routing(cap, ids, nums, yl, z)
+    for a, out in ((0, lo), (1, gt)):
+        total = jnp.zeros(out.shape, F32)
+        for k in range(CHUNKS):
+            total = total + lax.dot_general(picks[k][1 - a], home[a, k], ROWS_TOP, preferred_element_type=F32)
+        out[...] = total.astype(BF)
+    for copy in outs:
+        copy.wait()
+
+
 def kernel(cap, f, h,
-           meta, tok, gout, wg, wu, wd,
-           lo, gt, gg, gu, gd,
-           picks, sent, tbuf, gbuf, wgu, wdn, act_mine, act_theirs, hid, gact, pout, pback,
-           home, gwt, gdt, ss, rs, ls, *landings):
+           ids, nums, tok, gout, wg, wu, wd,
+           home, gg, gu, gd,
+           sent, tbuf, gbuf, wgu, wdn, act_mine, act_theirs, hid, gact, pout, pback,
+           gwt, gdt, ss, rs, ls, *landings):
     d2 = 8 * f
-    grp, col = lax.axis_index("grp"), lax.axis_index("col")
-    yl, z = grp // 4, grp % 4
-    zh, zl = z // 2, z % 2
-    yh, x, c = col // 8, (col // 2) % 4, col % 2
+    yl, z, yh, x, c = place()
+    zl = z % 2
     xr, xl, xo = (x + 1) % 4, (x + 3) % 4, (x + 2) % 4
 
     def dev(yl=yl, z=z, yh=yh, x=x, c=c):
@@ -69,9 +123,7 @@
     right, left = dev(x=xr), dev(x=xl)
     other_y, other_z, other_c = dev(yh=1 - yh), dev(z=z + 1 - 2 * zl), dev(c=1 - c)
 
-    def source(k):
-        dy, dz = k // 2, k % 2
-        return dict(yl=1 - yl if dy else yl, z=3 - z if dz else z)
+    homes = sources(yl, z)
 
     counter = [0]
     started = []
@@ -115,7 +167,7 @@
             dst[at] = total.astype(BF)
 
     barrier = pltpu.get_barrier_semaphore()
-    partners = [right, left, other_y, other_z, other_c] + [dev(**source(k)) for k in (1, 2, 3)]
+    partners = [right, left, other_y, other_z, other_c] + [dev(**homes[k]) for k in (1, 2, 3)]
     for partner in partners:
         pl.semaphore_signal(barrier, inc=1, device_id=partner, device_id_type=MESH)
 
@@ -148,28 +200,7 @@
         for i, part in ((0, half_gu), (1, half_gu), (2, half_gu), (3, half_d), (4, half_d), (5, half_d)):
             pltpu.make_async_copy(part, part, ls.at[i]).wait()
 
-    first, second = meta[0:1, :], meta[1:2, :]
-    share = meta[2:3, :].astype(F32) / 64.0
-    count = first.shape[1]
-    has, weight = [], []
-    for k in range(CHUNKS):
-        where = source(k)
-        expert = where["yl"] * 2 + where["z"] // 2
-        one, two = first == expert, second == expert
-        has.append(jnp.logical_or(one, two).astype(F32))
-        weight.append(jnp.where(one, share, 1.0 - share))
-    marks = jnp.concatenate(has + [jnp.zeros((4, count), F32)], axis=0)
-    before = (lax.broadcasted_iota(jnp.int32, (count, count), 0)
-              < lax.broadcasted_iota(jnp.int32, (count, count), 1)).astype(F32)
-    position = jnp.dot(marks.astype(BF), before.astype(BF), preferred_element_type=F32)
-    slot = lax.broadcasted_iota(jnp.int32, (cap, count), 0).astype(F32)
-    for k in range(CHUNKS):
-        chosen = jnp.where(slot == position[k:k + 1, :], has[k], 0.0)
-        picks[0, k] = chosen.astype(BF)
-        picks[1, k] = (chosen * weight[k]).astype(BF)
-        sent[0, k] = jnp.dot(picks[0, k], tok[...], preferred_element_type=F32).astype(BF)
-        sent[1, k] = jnp.dot(picks[1, k], gout[...], preferred_element_type=F32).astype(BF)
-
+    picks = routing(cap, ids, nums, yl, z)
     pend = {}
     two = 2 * cap
     bufs = (tbuf, gbuf)
@@ -197,13 +228,14 @@
     def dispatch(k, a):
         off = (off_a(x, yh), off_b(yh, x))[a]
         theirs = 1 - zl if k % 2 else zl
+        sent[a, k] = jnp.dot(picks[k][a], (tok, gout)[a][...], preferred_element_type=F32).astype(BF)
         dst = bufs[a].at[rws(k * two + theirs * cap, cap), lanes(off, f)]
         if k == 0:
             copy = pltpu.make_async_copy(sent.at[a, 0], dst, ls.at[6 + a])
             copy.start()
             pend["g", k, a] = [copy]
         else:
-            pend["g", k, a] = [send(sent.at[a, k], dst, dev(**source(k)))]
+            pend["g", k, a] = [send(sent.at[a, k], dst, dev(**homes[k]))]
 
     def gathered(k, a, phase):
         if phase == 0 and k == 0:
@@ -304,20 +336,20 @@
             swap_in(k, a, landing[k, a])
         axis, i, later = steps[phase - 1]
         first_x, axes = a == 1, REDUCE[a][k][:i]
-        place = functools.partial(region, first_x, k, axes)
+        spot = functools.partial(region, first_x, k, axes)
         if axis == "x":
-            up, down = place(x=xr if later else xo), place(x=xl if later else xo)
+            up, down = spot(x=xr if later else xo), spot(x=xl if later else xo)
             if not later:
                 up, down = halves(up)[0], halves(down)[1]
             moves = [(up, right), (down, left)]
             if later:
-                added = [(place(), (0, 1))]
+                added = [(spot(), (0, 1))]
             else:
-                added = [(halves(place(x=xr))[0], (0,)), (halves(place(x=xl))[1], (1,))]
+                added = [(halves(spot(x=xr))[0], (0,)), (halves(spot(x=xl))[1], (1,))]
         elif axis == "y":
-            moves, added = [(place(y=1 - yh), other_y)], [(place(), (0,))]
-        else:
-            moves, added = [(place(z=1 - zl), other_z)], [(place(), (0,))]
+            moves, added = [(spot(y=1 - yh), other_y)], [(spot(), (0,))]
+        else:
+            moves, added = [(spot(z=1 - zl), other_z)], [(spot(), (0,))]
         slots = inbox[k, a, phase]
         pend["r", k, a] = [send(view(sums[a], part), slot, target) for (part, target), slot in zip(moves, slots)]
         landing[k, a] = [(part, [slots[j] for j in which]) for part, which in added]
@@ -329,7 +361,7 @@
             copy = pltpu.make_async_copy(src, home.at[a, 0], ls.at[8 + a])
             copy.start()
         else:
-            copy = send(src, home.at[a, k], dev(**source(k)))
+            copy = send(src, home.at[a, k], dev(**homes[k]))
         pend["h", k, a] = copy
 
     def weight_grads_up(part):
@@ -366,21 +398,24 @@
     steps = dict(d=dispatch, g=gather, t=project_tokens, p=project_grads, s=swap, v=activate, o=expand_out,
                  b=expand_back, r=reduce, h=return_home, w=weight_grads_up, n=weight_grads_down)
     pl.semaphore_wait(barrier, len(partners))
-    weights_from_other()
-    for step in ORDER:
+    drained = 0
+    for i, step in enumerate(ORDER):
         steps[step[0]](*(int(digit) for digit in step[1:]))
+        if i == 11:
+            weights_from_other()
+        old = max(len(started) - 40, 0)
+        for copy in started[drained:old]:
+            copy.wait_send()
+        drained = old
     weight_grads_done()
-    for a, out in ((1, gt), (0, lo)):
-        total = jnp.zeros(out.shape, F32)
-        for k in range(CHUNKS):
+    for copy in started[drained:]:
+        copy.wait_send()
+    for k in range(CHUNKS):
+        for a in range(2):
             if k == 0:
                 pend["h", k, a].wait()
             else:
                 pend["h", k, a].wait_recv()
-            total = total + lax.dot_general(picks[1 - a, k], home[a, k], ROWS_TOP, preferred_element_type=F32)
-        out[...] = total.astype(BF)
-    for copy in started:
-        copy.wait_send()
 
 
 def body(tokens, grad_out, expert_ids, gate_num, gate_weight, up_weight, down_weight):
@@ -388,7 +423,7 @@
     d, h = gate_weight.shape
     cap = 5 * count // 8
     rows, d2 = 8 * cap, 8 * f
-    meta = jnp.concatenate([expert_ids.T, gate_num[None, :], jnp.zeros((5, count), jnp.int32)], axis=0)
+    ids, nums = expert_ids.T, gate_num.reshape(1, count)
     split = (2, 4, 2, f, h)
     vm = pl.BlockSpec(memory_space=pltpu.VMEM)
     anywhere = pl.BlockSpec(memory_space=pl.ANY)
@@ -396,28 +431,38 @@
     def v(*shape, dtype=BF):
         return pltpu.VMEM(shape, dtype)
 
+    def like(*shape):
+        return jax.ShapeDtypeStruct(shape, BF)
+
     sems = 112
-    lo, gt, gg, gu, gd = pl.pallas_call(
+    home, gg, gu, gd = pl.pallas_call(
         functools.partial(kernel, cap, f, h),
-        out_shape=(
-            jax.ShapeDtypeStruct((count, f), BF), jax.ShapeDtypeStruct((count, f), BF),
-            jax.ShapeDtypeStruct(split, BF), jax.ShapeDtypeStruct(split, BF),
-            jax.ShapeDtypeStruct((h, d), BF)),
-        in_specs=[vm, vm, vm, anywhere, anywhere, anywhere],
-        out_specs=(vm, vm, anywhere, anywhere, anywhere),
+        out_shape=(like(2, CHUNKS, cap, f), like(*split), like(*split), like(h, d)),
+        in_specs=[vm, vm, vm, vm, anywhere, anywhere, anywhere],
+        out_specs=(anywhere, anywhere, anywhere, anywhere),
         scratch_shapes=[
-            v(2, 4, cap, count), v(2, 4, cap, f), v(rows, d2), v(rows, d2),
+            v(2, CHUNKS, cap, f), v(rows, d2), v(rows, d2),
             v(4, 2, f, 4 * h), v(2 * h, d2),
             v(rows, 6 * h, dtype=F32), v(rows, 6 * h, dtype=F32), v(rows, 2 * h), v(rows, 4 * h),
             v(rows, d2), v(rows, d2),
-            v(2, 4, cap, f), v(4, 2, f, 4 * h), v(2 * h, d2),
+            v(4, 2, f, 4 * h), v(2 * h, d2),
             pltpu.SemaphoreType.DMA((sems,)), pltpu.SemaphoreType.DMA((sems,)), pltpu.SemaphoreType.DMA((16,)),
         ] + [v(*shape) for _, shape in boxes(cap, f)],
         compiler_params=pltpu.CompilerParams(
             collective_id=1, has_side_effects=True, vmem_limit_bytes=60 * 2**20),
         name="moe_layer",
-    )(meta, tokens, grad_out, gate_weight.reshape(split), up_weight.reshape(split), down_weight)
-    return lo, gt, gg.reshape(d, h), gu.reshape(d, h), gd
+    )(ids, nums, tokens, grad_out, gate_weight.reshape(split), up_weight.reshape(split), down_weight)
+
+    parts = 4
+    return tuple(pl.pallas_call(
+        functools.partial(finish, cap, parts),
+        out_shape=(like(count, f), like(count, f), like(d, h), like(d, h), like(h, d)),
+        in_specs=[vm, vm, vm, anywhere, anywhere, anywhere],
+        out_specs=(vm, vm, anywhere, anywhere, anywhere),
+        scratch_shapes=[v(2, d, h), v(h, d), pltpu.SemaphoreType.DMA((3, parts)), pltpu.SemaphoreType.DMA((3, parts))],
+        compiler_params=pltpu.CompilerParams(vmem_limit_bytes=60 * 2**20),
+        name="finish",
+    )(ids, nums, home, gg.reshape(d, h), gu.reshape(d, h), gd))
 
 
 def solution(mesh):

time: 125 us -> 118 us (0.944)
  local copies, waits for them, and re-layouts: 11.8 us -> 0 us
  Pallas kernels: 111 us -> 117 us
  other arithmetic: 1.36 us -> 0 us
    unnamed x9 -> x0, local copies, waits for them, and re-layouts: 11.7 us -> none
    pallas_call x1 -> x2, Pallas kernels: 111 us -> 117 us  [the longest x1 108 us: body(): pl.pallas_call(functools.partial(kernel, cap, f, h), out_shape=(like(2, C...]
    concatenate x1 -> x0, other arithmetic: 1.36 us -> none  [body(): jnp.concatenate([expert_ids.T, gate_num[None, :], jnp.zeros((5, count), j...]
where the time goes in v3:
time: 118 us; the launch traced here: 117 us
  Pallas kernels  117 us (99%)
    pallas_call x1, Pallas kernels, body(): pl.pallas_call(functools.partial(kernel, cap, f, h), out_shape=(like(2, C...  108 us
    pallas_call x1, Pallas kernels, body(): pl.pallas_call(functools.partial(finish, cap, parts), out_shape=(like(cou...  9.06 us

profile of v3, /device:TPU:0, one launch (start us, length us, event | category | flops | bytes accessed | tf_op | source)
XLA Modules:
  0.0 117.4 jit_solution(15433829622381485708)
XLA Ops:
  0.6 107.7 %moe_layer.1 = (bf16[2,4,80,384]{3,2,1,0:T(8,128)(2,1)}, bf16[2,4,2,384,256]{4,3,2,1,0:T(8,128)(2,1)}, bf16[2,4,2,384,256]{4,3,2,1,0:T(8,128)(2,1)}, bf16[256,6144]{1,0:T(8,128)(2,1)}) custom-call(s32[2,128]{1,0:T(2,128)} %bitcast.10, s32[1,128]{1,0:T(1,128)} %bitcast.12, bf16[128,384]{1,0:T(8,128)(2,1)} %tok.1, bf16[128,384]{1,0:T(8,128)(2,1)} %gout.1, ...), custom_call_target="tpu_custom_call" | custom-call | tf_op jit(solution)/shard_map/moe_layer/pallas_call | solution.py:438
  108.3 9.1 %finish.1 = (bf16[128,384]{1,0:T(8,128)(2,1)}, bf16[128,384]{1,0:T(8,128)(2,1)}, bf16[6144,256]{1,0:T(8,128)(2,1)}, bf16[6144,256]{1,0:T(8,128)(2,1)}, bf16[256,6144]{1,0:T(8,128)(2,1)}) custom-call(s32[2,128]{1,0:T(2,128)} %bitcast.11, s32[1,128]{1,0:T(1,128)} %bitcast.13, bf16[2,4,80,384]{3,2,1,0:T(8,128)(2,1)} %get-tuple-element.9.home, ...), custom_call_target="tpu_custom_call" | custom-call | tf_op jit(solution)/shard_map/finish/pallas_call | solution.py:457

commit v4 on v3

--- a/solution.py
+++ b/solution.py
@@ -13,37 +13,42 @@
 CHUNKS = 4
 ROWS_TOP = (((0,), (0,)), ((), ()))
 ROWS_BOTH = (((1,), (1,)), ((), ()))
-GATHER = (("zyx", "yzx", "zyx", "yzx"), ("xzy", "xyz", "xyz", "xzy"))
-REDUCE = (("zxy", "xzy", "xyz", "xyz"), ("yzx", "zyx", "yzx", "yzx"))
+GATHER = (("Myzx", "Mzyx", "Myzx", "Myzx"), ("Xyz", "Mzxy", "Xzy", "xyz"))
+REDUCE = (("xzy", "Xzy", "Xzy", "Xyz"), ("Mzyx", "Mzyx", "MyXz", "Myzx"))
 ORDER = (
-    "d31", "d00", "d01", "d21", "g001", "d20", "d10", "d11", "g011", "d30", "g311", "g002", "g101", "g211",
-    "g012", "g111", "g201", "g312", "g301", "g212", "g013", "g202", "g003", "g112", "g102", "g313", "g213", "g302",
-    "g203", "g014", "g004", "g113", "g103", "g214", "g204", "g314", "t0", "g303", "p0", "s0", "g104", "t2",
-    "g114", "v0", "b0", "g304", "p2", "r011", "s2", "o0", "t1", "r001", "t3", "v2", "o2", "r201",
-    "r012", "p3", "s3", "p1", "s1", "b2", "r211", "v3", "b3", "r311", "v1", "r013", "o1", "r101",
-    "r212", "o3", "r301", "r202", "b1", "r111", "r312", "r014", "r002", "w0", "r213", "n1", "n2", "r112",
-    "w2", "r102", "n0", "r302", "w3", "r313", "r214", "r003", "n3", "r203", "h01", "w1", "r113", "r103",
-    "r303", "r314", "r004", "r204", "h21", "r104", "r304", "r114", "h00", "h20", "h31", "h10", "h30", "h11",
+    "d21", "d01", "g011", "d31", "d00", "d20", "d11", "d10", "d30", "g211", "g012", "g311", "g001", "g111",
+    "g201", "g312", "g212", "g101", "g002", "g313", "g202", "g013", "g213", "g112", "g003", "g203", "g301", "g113",
+    "g102", "p0", "t0", "s0", "g302", "g314", "t2", "p2", "s2", "v0", "o0", "r001", "b0", "g103",
+    "r011", "v2", "b2", "r211", "g303", "p1", "o2", "t1", "s1", "r012", "r201", "p3", "t3", "s3",
+    "v1", "r002", "o1", "r101", "r212", "v3", "o3", "r301", "b3", "r311", "b1", "r111", "r202", "n1",
+    "r312", "n2", "w0", "r112", "r302", "w1", "r102", "r003", "r013", "n3", "r313", "r203", "w2", "r113",
+    "r303", "r103", "r004", "h21", "h01", "h20", "h31", "w3", "h11", "h30", "n0", "h10", "h00",
 )
+
+
+def gather_steps(path):
+    axes, steps = path.strip("M"), []
+    for i, axis in enumerate(axes):
+        if i or path[0] != "M":
+            steps += [(axis, axes[:i].lower(), later) for later in range(2 if axis == "x" else 1)]
+    return steps
+
+
+def reduce_steps(path):
+    steps = gather_steps(path)
+    return sorted(steps, key=lambda step: (-len(step[1]), step[2]))
 
 
 def boxes(cap, f):
     found = []
     for k in range(CHUNKS):
         for a in range(2):
-            phase = 0
-            for i in (2, 1, 0):
-                axis, axes = REDUCE[a][k][i], REDUCE[a][k][:i]
+            for i, (axis, axes, later) in enumerate(reduce_steps(REDUCE[a][k])):
                 n = 2 * cap if "z" in axes else cap
                 width = f * (4 if "x" in axes else 1) * (2 if "y" in axes else 1)
-                phase += 1
-                if axis == "x":
-                    top = -(-n // 32) * 16
-                    found += [((k, a, phase), (top, width)), ((k, a, phase), (n - top, width))]
-                    phase += 1
-                    found += [((k, a, phase), (n, width))] * 2
-                else:
-                    found.append(((k, a, phase), (n, width)))
+                top = -(-n // 32) * 16
+                rows = [n] * 3 if axis == "X" else [n] if axis != "x" else [n, n] if later else [top, n - top]
+                found += [((k, a, i + 1), (some, width)) for some in rows]
     return found
 
 
@@ -82,28 +87,25 @@
     return found
 
 
-def finish(cap, parts, ids, nums, home, gg, gu, gd, lo, gt, ggo, guo, gdo, tall, wide, into, out_of):
-    long, across = gg.shape[0] // parts, gd.shape[1] // parts
-    ins, outs = [], []
-    for i in range(parts):
-        rows, lanes = (pl.ds(i * long, long), slice(None)), (slice(None), pl.ds(i * across, across))
-        for q, (src, held, dst, at) in enumerate((
-                (gg, tall.at[0], ggo, rows), (gu, tall.at[1], guo, rows), (gd, wide, gdo, lanes))):
-            ins.append(pltpu.make_async_copy(src.at[at], held.at[at], into.at[q, i]))
-            outs.append(pltpu.make_async_copy(held.at[at], dst.at[at], out_of.at[q, i]))
-    for copy in ins:
+def finish(cap, parts, ids, nums, home, gg, gu, gd, lo, gt, ggo, guo, gdo, done):
+    copies = []
+    for q, (src, dst) in enumerate(((gg, ggo), (gu, guo), (gd, gdo))):
+        rows = src.shape[0] // parts
+        for i in range(parts):
+            at = pl.ds(i * rows, rows)
+            copies.append(pltpu.make_async_copy(src.at[at], dst.at[at], done.at[q, i]))
+    for copy in copies:
         copy.start()
-    for landed, leaving in zip(ins, outs):
-        landed.wait()
-        leaving.start()
     yl, z, _, _, _ = place()
     picks = routing(cap, ids, nums, yl, z)
     for a, out in ((0, lo), (1, gt)):
         total = jnp.zeros(out.shape, F32)
         for k in range(CHUNKS):
-            total = total + lax.dot_general(picks[k][1 - a], home[a, k], ROWS_TOP, preferred_element_type=F32)
+            for part in range(2 if REDUCE[a][k][0] == "M" else 1):
+                total = total + lax.dot_general(
+                    picks[k][1 - a], home[a, k, part], ROWS_TOP, preferred_element_type=F32)
         out[...] = total.astype(BF)
-    for copy in outs:
+    for copy in copies:
         copy.wait()
 
 
@@ -125,6 +127,12 @@
 
     homes = sources(yl, z)
 
+    def beside(k, axis):
+        if axis == "y":
+            return dev(**homes[k], yh=1 - yh)
+        there = homes[k]["z"]
+        return dev(yl=homes[k]["yl"], z=there + 1 - 2 * (there % 2))
+
     counter = [0]
     started = []
     inbox, landing = {}, {}
@@ -167,7 +175,10 @@
             dst[at] = total.astype(BF)
 
     barrier = pltpu.get_barrier_semaphore()
-    partners = [right, left, other_y, other_z, other_c] + [dev(**homes[k]) for k in (1, 2, 3)]
+    across = dev(x=xo)
+    partners = [right, left, across, other_y, other_z, other_c]
+    partners += [dev(**homes[k]) for k in (1, 2, 3)]
+    partners += [beside(k, axis) for axis, ks in (("y", (1, 2, 3)), ("z", (1,))) for k in ks]
     for partner in partners:
         pl.semaphore_signal(barrier, inc=1, device_id=partner, device_id_type=MESH)
 
@@ -201,7 +212,7 @@
             pltpu.make_async_copy(part, part, ls.at[i]).wait()
 
     picks = routing(cap, ids, nums, yl, z)
-    pend = {}
+    pend, local = {}, {}
     two = 2 * cap
     bufs = (tbuf, gbuf)
     sums = (pout, pback)
@@ -233,34 +244,34 @@
         if k == 0:
             copy = pltpu.make_async_copy(sent.at[a, 0], dst, ls.at[6 + a])
             copy.start()
-            pend["g", k, a] = [copy]
+            local["d", a] = copy
+            pend["g", k, a] = []
         else:
             pend["g", k, a] = [send(sent.at[a, k], dst, dev(**homes[k]))]
-
-    def gathered(k, a, phase):
-        if phase == 0 and k == 0:
-            pend["g", k, a][0].wait()
-        else:
-            got(pend["g", k, a])
+        path = GATHER[a][k]
+        if path[0] == "M":
+            pend["g", k, a].append(send(sent.at[a, k], dst, beside(k, path[1])))
+
+    def gathered(k, a):
+        if k == 0 and ("d", a) in local:
+            local.pop(("d", a)).wait()
+        got(pend["g", k, a])
 
     def gather(k, a, phase):
-        gathered(k, a, phase - 1)
-        steps = []
-        for i, axis in enumerate(GATHER[a][k]):
-            steps += [(axis, i, 0), (axis, i, 1)] if axis == "x" else [(axis, i, 0)]
-        axis, i, later = steps[phase - 1]
-        buf, axes = bufs[a], GATHER[a][k][:i]
+        gathered(k, a)
+        axis, axes, later = gather_steps(GATHER[a][k])[phase - 1]
+        buf = bufs[a]
         if axis == "x" and later:
             up = view(buf, halves(region(a == 0, k, axes, x=xl))[0])
             down = view(buf, halves(region(a == 0, k, axes, x=xr))[1])
             pend["g", k, a] = [send(up, up, right), send(down, down, left)]
         else:
             mine = view(buf, region(a == 0, k, axes))
-            to = (right, left) if axis == "x" else (other_y,) if axis == "y" else (other_z,)
+            to = dict(x=(right, left), X=(right, left, across), y=(other_y,), z=(other_z,))[axis]
             pend["g", k, a] = [send(mine, mine, target) for target in to]
 
     def project_tokens(k):
-        gathered(k, 0, 4)
+        gathered(k, 0)
         rows = pl.ds(k * two, two)
         if not ready:
             weights_ready()
@@ -272,7 +283,7 @@
             act_mine[rows, lanes(n * 2 * h, 2 * h)] = jnp.dot(tbuf[rows, :], w, preferred_element_type=F32)
 
     def project_grads(k):
-        gathered(k, 1, 4)
+        gathered(k, 1)
         rows = pl.ds(k * two, two)
         if not ready:
             weights_ready()
@@ -328,71 +339,71 @@
             add_into(sums[a], row, n, off, width, *slots)
 
     def reduce(k, a, phase):
-        steps = []
-        for i in (2, 1, 0):
-            axis = REDUCE[a][k][i]
-            steps += [(axis, i, 0), (axis, i, 1)] if axis == "x" else [(axis, i, 0)]
         if phase > 1:
             swap_in(k, a, landing[k, a])
-        axis, i, later = steps[phase - 1]
-        first_x, axes = a == 1, REDUCE[a][k][:i]
-        spot = functools.partial(region, first_x, k, axes)
-        if axis == "x":
-            up, down = spot(x=xr if later else xo), spot(x=xl if later else xo)
-            if not later:
-                up, down = halves(up)[0], halves(down)[1]
-            moves = [(up, right), (down, left)]
-            if later:
-                added = [(spot(), (0, 1))]
-            else:
-                added = [(halves(spot(x=xr))[0], (0,)), (halves(spot(x=xl))[1], (1,))]
+        axis, axes, later = reduce_steps(REDUCE[a][k])[phase - 1]
+        spot = functools.partial(region, a == 1, k, axes)
+        slots = inbox[k, a, phase]
+        if axis == "X":
+            moves = [(spot(x=xr), right), (spot(x=xl), left), (spot(x=xo), across)]
+            added = [(spot(), (0, 1, 2))]
+        elif axis == "x" and later:
+            moves, added = [(spot(x=xr), right), (spot(x=xl), left)], [(spot(), (0, 1))]
+        elif axis == "x":
+            moves = [(halves(spot(x=xo))[0], right), (halves(spot(x=xo))[1], left)]
+            added = [(halves(spot(x=xr))[0], (0,)), (halves(spot(x=xl))[1], (1,))]
         elif axis == "y":
             moves, added = [(spot(y=1 - yh), other_y)], [(spot(), (0,))]
         else:
             moves, added = [(spot(z=1 - zl), other_z)], [(spot(), (0,))]
-        slots = inbox[k, a, phase]
         pend["r", k, a] = [send(view(sums[a], part), slot, target) for (part, target), slot in zip(moves, slots)]
         landing[k, a] = [(part, [slots[j] for j in which]) for part, which in added]
 
     def return_home(k, a):
         swap_in(k, a, landing[k, a])
-        src = view(sums[a], region(a == 1, k, ""))
+        spot = functools.partial(region, a == 1, k, "")
+        mine, path = view(sums[a], spot()), REDUCE[a][k]
+        pend["h", k, a] = []
         if k == 0:
-            copy = pltpu.make_async_copy(src, home.at[a, 0], ls.at[8 + a])
-            copy.start()
+            local["h", a] = pltpu.make_async_copy(mine, home.at[a, 0, 0], ls.at[8 + a])
+            local["h", a].start()
         else:
-            copy = send(src, home.at[a, k], dev(**homes[k]))
-        pend["h", k, a] = copy
+            pend["h", k, a].append(send(mine, home.at[a, k, 0], dev(**homes[k])))
+        if path[0] == "M":
+            theirs = view(sums[a], spot(y=1 - yh) if path[1] == "y" else spot(z=1 - zl))
+            pend["h", k, a].append(send(theirs, home.at[a, k, 1], beside(k, path[1])))
 
     def weight_grads_up(part):
         @pl.loop(part * 2, part * 2 + 2)
         def _(p):
-            xx, yy = p // 2, p % 2
-            gwt[xx, yy] = lax.dot_general(
-                tbuf[:, lanes(p * f, f)], gact[...], ROWS_TOP, preferred_element_type=F32).astype(BF)
+            there = rws((((p % 2) * 4 + p // 2) * 2 + c) * f, f)
             for q, out in enumerate((gg, gu)):
-                pltpu.make_async_copy(
-                    gwt.at[xx, yy, :, lanes(2 * h * q + h * c, h)], out.at[yy, xx, c], ls.at[10]).start()
+                def product(core):
+                    return lax.dot_general(
+                        tbuf[:, lanes(p * f, f)], gact[:, lanes(2 * h * q + h * core, h)], ROWS_TOP,
+                        preferred_element_type=F32).astype(BF)
+                gwt[q, p] = product(1 - c)
                 pltpu.make_async_remote_copy(
-                    src_ref=gwt.at[xx, yy, :, lanes(2 * h * q + h * (1 - c), h)], dst_ref=out.at[yy, xx, c],
-                    send_sem=ls.at[11], recv_sem=ls.at[12], device_id=other_c, device_id_type=MESH).start()
+                    src_ref=gwt.at[q, p], dst_ref=out.at[there], send_sem=ls.at[11], recv_sem=ls.at[12],
+                    device_id=other_c, device_id_type=MESH).start()
+                out[there, :] = product(c)
 
     def weight_grads_down(part):
         @pl.loop(part * 2, part * 2 + 2)
         def _(p):
-            at = lanes(p * f, f)
-            gdt[:, at] = lax.dot_general(
-                hid[...], gbuf[:, at], ROWS_TOP, preferred_element_type=F32).astype(BF)
             there = lanes((p * 2 + c) * f, f)
-            pltpu.make_async_copy(gdt.at[rws(h * c, h), at], gd.at[:, there], ls.at[13]).start()
+            def product(core):
+                return lax.dot_general(
+                    hid[:, lanes(h * core, h)], gbuf[:, lanes(p * f, f)], ROWS_TOP,
+                    preferred_element_type=F32).astype(BF)
+            gdt[p] = product(1 - c)
             pltpu.make_async_remote_copy(
-                src_ref=gdt.at[rws(h * (1 - c), h), at], dst_ref=gd.at[:, there],
-                send_sem=ls.at[14], recv_sem=ls.at[15], device_id=other_c, device_id_type=MESH).start()
+                src_ref=gdt.at[p], dst_ref=gd.at[:, there], send_sem=ls.at[14], recv_sem=ls.at[15],
+                device_id=other_c, device_id_type=MESH).start()
+            gd[:, there] = product(c)
 
     def weight_grads_done():
-        half_gu = gwt.at[:, :, :, pl.ds(0, 2 * h)]
-        half_d = gdt.at[pl.ds(0, h)]
-        for i, part in ((10, half_gu), (11, half_gu), (12, half_gu), (13, half_d), (14, half_d), (15, half_d)):
+        for i, part in ((11, gwt), (12, gwt), (14, gdt), (15, gdt)):
             pltpu.make_async_copy(part, part, ls.at[i]).wait()
 
     steps = dict(d=dispatch, g=gather, t=project_tokens, p=project_grads, s=swap, v=activate, o=expand_out,
@@ -410,12 +421,10 @@
     weight_grads_done()
     for copy in started[drained:]:
         copy.wait_send()
-    for k in range(CHUNKS):
-        for a in range(2):
-            if k == 0:
-                pend["h", k, a].wait()
-            else:
-                pend["h", k, a].wait_recv()
+    for a in range(2):
+        local["h", a].wait()
+        for k in range(CHUNKS):
+            got(pend["h", k, a])
 
 
 def body(tokens, grad_out, expert_ids, gate_num, gate_weight, up_weight, down_weight):
@@ -434,22 +443,22 @@
     def like(*shape):
         return jax.ShapeDtypeStruct(shape, BF)
 
-    sems = 112
+    sems = 128
     home, gg, gu, gd = pl.pallas_call(
         functools.partial(kernel, cap, f, h),
-        out_shape=(like(2, CHUNKS, cap, f), like(*split), like(*split), like(h, d)),
+        out_shape=(v(2, CHUNKS, 2, cap, f), v(d, h), v(d, h), v(h, d)),
         in_specs=[vm, vm, vm, vm, anywhere, anywhere, anywhere],
-        out_specs=(anywhere, anywhere, anywhere, anywhere),
+        out_specs=(vm, vm, vm, vm),
         scratch_shapes=[
             v(2, CHUNKS, cap, f), v(rows, d2), v(rows, d2),
             v(4, 2, f, 4 * h), v(2 * h, d2),
             v(rows, 6 * h, dtype=F32), v(rows, 6 * h, dtype=F32), v(rows, 2 * h), v(rows, 4 * h),
             v(rows, d2), v(rows, d2),
-            v(4, 2, f, 4 * h), v(2 * h, d2),
+            v(2, 8, f, h), v(8, h, f),
             pltpu.SemaphoreType.DMA((sems,)), pltpu.SemaphoreType.DMA((sems,)), pltpu.SemaphoreType.DMA((16,)),
         ] + [v(*shape) for _, shape in boxes(cap, f)],
         compiler_params=pltpu.CompilerParams(
-            collective_id=1, has_side_effects=True, vmem_limit_bytes=60 * 2**20),
+            collective_id=1, has_side_effects=True, vmem_limit_bytes=49 * 2**20),
         name="moe_layer",
     )(ids, nums, tokens, grad_out, gate_weight.reshape(split), up_weight.reshape(split), down_weight)
 
@@ -457,12 +466,12 @@
     return tuple(pl.pallas_call(
         functools.partial(finish, cap, parts),
         out_shape=(like(count, f), like(count, f), like(d, h), like(d, h), like(h, d)),
-        in_specs=[vm, vm, vm, anywhere, anywhere, anywhere],
+        in_specs=[vm, vm, vm, vm, vm, vm],
         out_specs=(vm, vm, anywhere, anywhere, anywhere),
-        scratch_shapes=[v(2, d, h), v(h, d), pltpu.SemaphoreType.DMA((3, parts)), pltpu.SemaphoreType.DMA((3, parts))],
-        compiler_params=pltpu.CompilerParams(vmem_limit_bytes=60 * 2**20),
+        scratch_shapes=[pltpu.SemaphoreType.DMA((3, parts))],
+        compiler_params=pltpu.CompilerParams(vmem_limit_bytes=16 * 2**20),
         name="finish",
-    )(ids, nums, home, gg.reshape(d, h), gu.reshape(d, h), gd))
+    )(ids, nums, home, gg, gu, gd))
 
 
 def solution(mesh):

time: 118 us -> 112 us (0.949)
  Pallas kernels: 117 us -> 111 us
    pallas_call x1, Pallas kernels: 9.06 us -> 4.43 us  [body(): pl.pallas_call(functools.partial(finish, cap, parts), out_shape=(like(cou...]
    pallas_call x1, Pallas kernels: 108 us -> 106 us  [body(): pl.pallas_call(functools.partial(kernel, cap, f, h), out_shape=(v(2, CHUN...]
where the time goes in v4:
time: 112 us
  Pallas kernels  111 us (99%)
    pallas_call x1, Pallas kernels, body(): pl.pallas_call(functools.partial(kernel, cap, f, h), out_shape=(v(2, CHUN...  106 us
    pallas_call x1, Pallas kernels, body(): pl.pallas_call(functools.partial(finish, cap, parts), out_shape=(like(cou...  4.43 us

profile of v4, /device:TPU:0, one launch (start us, length us, event | category | flops | bytes accessed | tf_op | source)
XLA Modules:
  0.0 111.8 jit_solution(1892627789260174246)
XLA Ops:
  0.6 0.0 copy-start
  0.6 0.0 copy-start.1
  0.7 106.5 %moe_layer.1 = (bf16[2,4,2,80,384]{4,3,2,1,0:T(8,128)(2,1)S(1)}, bf16[6144,256]{1,0:T(8,128)(2,1)S(1)}, bf16[6144,256]{1,0:T(8,128)(2,1)S(1)}, bf16[256,6144]{1,0:T(8,128)(2,1)S(1)}) custom-call(s32[2,128]{1,0:T(2,128)} %bitcast.4, s32[1,128]{1,0:T(1,128)} %bitcast.6, bf16[128,384]{1,0:T(8,128)(2,1)} %tok.1, bf16[128,384]{1,0:T(8,128)(2,1)} %gout.1, ...), custom_call_target="tpu_custom_call" | custom-call | tf_op jit(solution)/shard_map/moe_layer/pallas_call | solution.py:447
  107.1 0.0 copy-done
  107.2 0.0 copy-done.1
  107.2 4.4 %finish.1 = (bf16[128,384]{1,0:T(8,128)(2,1)}, bf16[128,384]{1,0:T(8,128)(2,1)}, bf16[6144,256]{1,0:T(8,128)(2,1)}, bf16[6144,256]{1,0:T(8,128)(2,1)}, bf16[256,6144]{1,0:T(8,128)(2,1)}) custom-call(s32[2,128]{1,0:T(2,128)S(1)} %bitcast.5, s32[1,128]{1,0:T(1,128)S(1)} %bitcast.7, bf16[2,4,2,80,384]{4,3,2,1,0:T(8,128)(2,1)S(1)} %get-tuple-element.9.home, ...), custom_call_target="tpu_custom_call" | custom-call | tf_op jit(solution)/shard_map/finish/pallas_call | solution.py:466
Async XLA Ops:
  0.6 106.5 %copy-start = (s32[128,2]{0,1:T(2,128)S(1)}, s32[128,2]{0,1:T(2,128)}, u32[]{:S(2)}) copy-start(s32[128,2]{0,1:T(2,128)} %param.9) | copy-start | bytes 3076
  0.6 106.5 %copy-start.1 = (s32[128]{0:T(128)S(1)}, s32[128]{0:T(128)}, u32[]{:S(2)}) copy-start(s32[128]{0:T(128)} %param.10) | copy-start | bytes 1540

commit v5 on v4

--- a/solution.py
+++ b/solution.py
@@ -13,16 +13,17 @@
 CHUNKS = 4
 ROWS_TOP = (((0,), (0,)), ((), ()))
 ROWS_BOTH = (((1,), (1,)), ((), ()))
-GATHER = (("Myzx", "Mzyx", "Myzx", "Myzx"), ("Xyz", "Mzxy", "Xzy", "xyz"))
-REDUCE = (("xzy", "Xzy", "Xzy", "Xyz"), ("Mzyx", "Mzyx", "MyXz", "Myzx"))
+GATHER = (("yzx", "zyx", "zyx", "yzx"), ("Xyz", "Xzy", "xyz", "zxy"))
+REDUCE = (("xyz", "Xyz", "Xzy", "Xyz"), ("Mzyx", "Mzyx", "Myzx", "Myzx"))
 ORDER = (
-    "d21", "d01", "g011", "d31", "d00", "d20", "d11", "d10", "d30", "g211", "g012", "g311", "g001", "g111",
-    "g201", "g312", "g212", "g101", "g002", "g313", "g202", "g013", "g213", "g112", "g003", "g203", "g301", "g113",
-    "g102", "p0", "t0", "s0", "g302", "g314", "t2", "p2", "s2", "v0", "o0", "r001", "b0", "g103",
-    "r011", "v2", "b2", "r211", "g303", "p1", "o2", "t1", "s1", "r012", "r201", "p3", "t3", "s3",
-    "v1", "r002", "o1", "r101", "r212", "v3", "o3", "r301", "b3", "r311", "b1", "r111", "r202", "n1",
-    "r312", "n2", "w0", "r112", "r302", "w1", "r102", "r003", "r013", "n3", "r313", "r203", "w2", "r113",
-    "r303", "r103", "r004", "h21", "h01", "h20", "h31", "w3", "h11", "h30", "n0", "h10", "h00",
+    "d00", "d01", "g001", "d11", "g011", "d21", "d31", "d20", "d10", "g002", "g111", "g101", "g012", "g211",
+    "g311", "g201", "g003", "d30", "g112", "g102", "g212", "g312", "g013", "g202", "g301", "g004", "g103", "g213",
+    "g203", "g113", "t0", "g313", "g302", "g214", "p0", "s0", "g104", "g204", "g303", "v0", "o0", "b0",
+    "g314", "r001", "t1", "p1", "s1", "r011", "t2", "p2", "s2", "v1", "g304", "b1", "r111", "v2",
+    "o2", "r201", "r012", "o1", "r101", "t3", "r002", "p3", "s3", "r112", "b2", "v3", "o3", "r301",
+    "r211", "b3", "r311", "r102", "n0", "r212", "w0", "r202", "r113", "r312", "r003", "w3", "r302", "n3",
+    "r013", "r103", "r213", "n1", "n2", "r203", "r313", "w1", "r303", "h21", "h10", "h11", "r004", "h31",
+    "h20", "w2", "h01", "h30", "h00",
 )
 
 
@@ -112,7 +113,7 @@
 def kernel(cap, f, h,
            ids, nums, tok, gout, wg, wu, wd,
            home, gg, gu, gd,
-           sent, tbuf, gbuf, wgu, wdn, act_mine, act_theirs, hid, gact, pout, pback,
+           tok_in, gout_in, sent, tbuf, gbuf, wgu, wdn, act_mine, act_theirs, hid, gact, pout, pback,
            gwt, gdt, ss, rs, ls, *landings):
     d2 = 8 * f
     yl, z, yh, x, c = place()
@@ -181,6 +182,11 @@
     partners += [beside(k, axis) for axis, ks in (("y", (1, 2, 3)), ("z", (1,))) for k in ks]
     for partner in partners:
         pl.semaphore_signal(barrier, inc=1, device_id=partner, device_id_type=MESH)
+
+    taken = [pltpu.make_async_copy(src, dst, ls.at[10 + 3 * i])
+             for i, (src, dst) in enumerate(((tok, tok_in), (gout, gout_in)))]
+    for copy in taken:
+        copy.start()
 
     for y in range(2):
         for q, w in enumerate((wg, wu)):
@@ -212,6 +218,8 @@
             pltpu.make_async_copy(part, part, ls.at[i]).wait()
 
     picks = routing(cap, ids, nums, yl, z)
+    for copy in taken:
+        copy.wait()
     pend, local = {}, {}
     two = 2 * cap
     bufs = (tbuf, gbuf)
@@ -239,7 +247,7 @@
     def dispatch(k, a):
         off = (off_a(x, yh), off_b(yh, x))[a]
         theirs = 1 - zl if k % 2 else zl
-        sent[a, k] = jnp.dot(picks[k][a], (tok, gout)[a][...], preferred_element_type=F32).astype(BF)
+        sent[a, k] = jnp.dot(picks[k][a], (tok_in, gout_in)[a][...], preferred_element_type=F32).astype(BF)
         dst = bufs[a].at[rws(k * two + theirs * cap, cap), lanes(off, f)]
         if k == 0:
             copy = pltpu.make_async_copy(sent.at[a, 0], dst, ls.at[6 + a])
@@ -447,10 +455,10 @@
     home, gg, gu, gd = pl.pallas_call(
         functools.partial(kernel, cap, f, h),
         out_shape=(v(2, CHUNKS, 2, cap, f), v(d, h), v(d, h), v(h, d)),
-        in_specs=[vm, vm, vm, vm, anywhere, anywhere, anywhere],
+        in_specs=[vm, vm, anywhere, anywhere, anywhere, anywhere, anywhere],
         out_specs=(vm, vm, vm, vm),
         scratch_shapes=[
-            v(2, CHUNKS, cap, f), v(rows, d2), v(rows, d2),
+            v(count, f), v(count, f), v(2, CHUNKS, cap, f), v(rows, d2), v(rows, d2),
             v(4, 2, f, 4 * h), v(2 * h, d2),
             v(rows, 6 * h, dtype=F32), v(rows, 6 * h, dtype=F32), v(rows, 2 * h), v(rows, 4 * h),
             v(rows, d2), v(rows, d2),

time: 112 us -> 109 us (0.973)
  Pallas kernels: 111 us -> 108 us
    pallas_call x1, Pallas kernels: 106 us -> 103 us  [body(): pl.pallas_call(functools.partial(kernel, cap, f, h), out_shape=(v(2, CHUN...]
where the time goes in v5:
time: 109 us
  Pallas kernels  108 us (99%)
    pallas_call x1, Pallas kernels, body(): pl.pallas_call(functools.partial(kernel, cap, f, h), out_shape=(v(2, CHUN...  103 us
    pallas_call x1, Pallas kernels, body(): pl.pallas_call(functools.partial(finish, cap, parts), out_shape=(like(cou...  4.43 us

profile of v5, /device:TPU:0, one launch (start us, length us, event | category | flops | bytes accessed | tf_op | source)
XLA Modules:
  0.0 108.5 jit_solution(17837959509586152216)
XLA Ops:
  0.6 0.0 copy-start
  0.6 0.0 copy-start.1
  0.7 103.3 %moe_layer.1 = (bf16[2,4,2,80,384]{4,3,2,1,0:T(8,128)(2,1)S(1)}, bf16[6144,256]{1,0:T(8,128)(2,1)S(1)}, bf16[6144,256]{1,0:T(8,128)(2,1)S(1)}, bf16[256,6144]{1,0:T(8,128)(2,1)S(1)}) custom-call(s32[2,128]{1,0:T(2,128)} %bitcast.4, s32[1,128]{1,0:T(1,128)} %bitcast.6, bf16[128,384]{1,0:T(8,128)(2,1)} %tok.1, bf16[128,384]{1,0:T(8,128)(2,1)} %gout.1, ...), custom_call_target="tpu_custom_call" | custom-call | tf_op jit(solution)/shard_map/moe_layer/pallas_call | solution.py:455
  103.9 0.0 copy-done
  103.9 0.0 copy-done.1
  103.9 4.4 %finish.1 = (bf16[128,384]{1,0:T(8,128)(2,1)}, bf16[128,384]{1,0:T(8,128)(2,1)}, bf16[6144,256]{1,0:T(8,128)(2,1)}, bf16[6144,256]{1,0:T(8,128)(2,1)}, bf16[256,6144]{1,0:T(8,128)(2,1)}) custom-call(s32[2,128]{1,0:T(2,128)S(1)} %bitcast.5, s32[1,128]{1,0:T(1,128)S(1)} %bitcast.7, bf16[2,4,2,80,384]{4,3,2,1,0:T(8,128)(2,1)S(1)} %get-tuple-element.9.home, ...), custom_call_target="tpu_custom_call" | custom-call | tf_op jit(solution)/shard_map/finish/pallas_call | solution.py:474
Async XLA Ops:
  0.6 103.3 %copy-start = (s32[128,2]{0,1:T(2,128)S(1)}, s32[128,2]{0,1:T(2,128)}, u32[]{:S(2)}) copy-start(s32[128,2]{0,1:T(2,128)} %param.9) | copy-start | bytes 3076
  0.6 103.3 %copy-start.1 = (s32[128]{0:T(128)S(1)}, s32[128]{0:T(128)}, u32[]{:S(2)}) copy-start(s32[128]{0:T(128)} %param.10) | copy-start | bytes 1540

commit v6 on v5

--- a/solution.py
+++ b/solution.py
@@ -13,17 +13,17 @@
 CHUNKS = 4
 ROWS_TOP = (((0,), (0,)), ((), ()))
 ROWS_BOTH = (((1,), (1,)), ((), ()))
-GATHER = (("yzx", "zyx", "zyx", "yzx"), ("Xyz", "Xzy", "xyz", "zxy"))
-REDUCE = (("xyz", "Xyz", "Xzy", "Xyz"), ("Mzyx", "Mzyx", "Myzx", "Myzx"))
+GATHER = (("zyx", "yzx", "Myzx", "zyx"), ("Xzy", "xyz", "Xyz", "xzy"))
+REDUCE = (("Xzy", "Mzxy", "xyz", "Xyz"), ("Myzx", "Mzyx", "Myzx", "Myzx"))
 ORDER = (
-    "d00", "d01", "g001", "d11", "g011", "d21", "d31", "d20", "d10", "g002", "g111", "g101", "g012", "g211",
-    "g311", "g201", "g003", "d30", "g112", "g102", "g212", "g312", "g013", "g202", "g301", "g004", "g103", "g213",
-    "g203", "g113", "t0", "g313", "g302", "g214", "p0", "s0", "g104", "g204", "g303", "v0", "o0", "b0",
-    "g314", "r001", "t1", "p1", "s1", "r011", "t2", "p2", "s2", "v1", "g304", "b1", "r111", "v2",
-    "o2", "r201", "r012", "o1", "r101", "t3", "r002", "p3", "s3", "r112", "b2", "v3", "o3", "r301",
-    "r211", "b3", "r311", "r102", "n0", "r212", "w0", "r202", "r113", "r312", "r003", "w3", "r302", "n3",
-    "r013", "r103", "r213", "n1", "n2", "r203", "r313", "w1", "r303", "h21", "h10", "h11", "r004", "h31",
-    "h20", "w2", "h01", "h30", "h00",
+    "d21", "d00", "d01", "d31", "g001", "g011", "d11", "d10", "d20", "g002", "g211", "g012", "g311", "g101",
+    "g201", "g111", "d30", "g212", "g003", "g013", "g112", "g301", "g312", "g102", "g202", "g213", "g302", "g313",
+    "g004", "g113", "g203", "g103", "t0", "p0", "s0", "t2", "g303", "p2", "s2", "v0", "o0", "g314",
+    "g114", "g104", "b0", "v2", "r011", "g304", "r001", "b2", "o2", "r211", "r201", "r012", "t1", "p1",
+    "s1", "t3", "r212", "p3", "v1", "s3", "o1", "r101", "b1", "r111", "v3", "o3", "r301", "b3",
+    "r311", "r202", "r013", "r112", "w3", "r213", "w0", "r102", "r312", "r002", "r302", "w2", "n2", "r203",
+    "r103", "r113", "n3", "n0", "r313", "r204", "h21", "h01", "r303", "h10", "r003", "h11", "h31", "h20",
+    "w1", "h30", "n1", "h00",
 )
 
 

time: 109 us -> 108 us (level)
  no operation moved by 1% of the time
where the time goes in v6:
time: 108 us
  Pallas kernels  107 us (99%)
    pallas_call x1, Pallas kernels, body(): pl.pallas_call(functools.partial(kernel, cap, f, h), out_shape=(v(2, CHUN...  103 us
    pallas_call x1, Pallas kernels, body(): pl.pallas_call(functools.partial(finish, cap, parts), out_shape=(like(cou...  4.43 us

profile of v6, /device:TPU:0, one launch (start us, length us, event | category | flops | bytes accessed | tf_op | source)
XLA Modules:
  0.0 108.0 jit_solution(16449841643125335860)
XLA Ops:
  0.6 0.0 copy-start
  0.6 0.0 copy-start.1
  0.7 102.8 %moe_layer.1 = (bf16[2,4,2,80,384]{4,3,2,1,0:T(8,128)(2,1)S(1)}, bf16[6144,256]{1,0:T(8,128)(2,1)S(1)}, bf16[6144,256]{1,0:T(8,128)(2,1)S(1)}, bf16[256,6144]{1,0:T(8,128)(2,1)S(1)}) custom-call(s32[2,128]{1,0:T(2,128)} %bitcast.4, s32[1,128]{1,0:T(1,128)} %bitcast.6, bf16[128,384]{1,0:T(8,128)(2,1)} %tok.1, bf16[128,384]{1,0:T(8,128)(2,1)} %gout.1, ...), custom_call_target="tpu_custom_call" | custom-call | tf_op jit(solution)/shard_map/moe_layer/pallas_call | solution.py:455
  103.4 0.0 copy-done
  103.4 0.0 copy-done.1
  103.5 4.4 %finish.1 = (bf16[128,384]{1,0:T(8,128)(2,1)}, bf16[128,384]{1,0:T(8,128)(2,1)}, bf16[6144,256]{1,0:T(8,128)(2,1)}, bf16[6144,256]{1,0:T(8,128)(2,1)}, bf16[256,6144]{1,0:T(8,128)(2,1)}) custom-call(s32[2,128]{1,0:T(2,128)S(1)} %bitcast.5, s32[1,128]{1,0:T(1,128)S(1)} %bitcast.7, bf16[2,4,2,80,384]{4,3,2,1,0:T(8,128)(2,1)S(1)} %get-tuple-element.9.home, ...), custom_call_target="tpu_custom_call" | custom-call | tf_op jit(solution)/shard_map/finish/pallas_call | solution.py:474
Async XLA Ops:
  0.6 102.8 %copy-start = (s32[128,2]{0,1:T(2,128)S(1)}, s32[128,2]{0,1:T(2,128)}, u32[]{:S(2)}) copy-start(s32[128,2]{0,1:T(2,128)} %param.9) | copy-start | bytes 3076
  0.6 102.8 %copy-start.1 = (s32[128]{0:T(128)S(1)}, s32[128]{0:T(128)}, u32[]{:S(2)}) copy-start(s32[128]{0:T(128)} %param.10) | copy-start | bytes 1540
